TPU v7x, 128 devices: a whole 4x4x4 slice. The times are simulated.
128 devices in a mesh: grp: 8 (over z_lo, y), seq: 16 (over z_hi, x, core).
Axes of the slice: x: 4, y: 4, z: 4 (z_hi: 2, z_lo: 2; z = z_hi * 2 + z_lo), core: 2. Of those that a mesh axis runs over, the one named last changes fastest.
Arguments:
- qkv: bfloat16 [32, 1024, 6144], P('grp', 'seq'), may hold values from -20 to 20
- text_kv: bfloat16 [32, 256, 4096], P('grp', 'seq'), may hold values from -6 to 6
- clip_blocks: int32 [32], replicated, may hold values from 1 to 4, as said below
- text_count: int32 [32], replicated, may hold values from 1 to 256, as said below
- dest_group: int32 [32], replicated, may hold values from 0 to 7, as said below
- out_weight: bfloat16 [2048, 3072], replicated, may hold values from -0.125 to 0.125
- grad_out: bfloat16 [32, 1024, 3072], P('grp', 'seq'), may hold values from -6 to 6
Outputs:
- out: bfloat16 [32, 1024, 3072], P('grp', 'seq')
- grad_qkv: bfloat16 [32, 1024, 6144], P('grp', 'seq')
- grad_text: bfloat16 [32, 256, 4096], P('grp', 'seq')
- grad_weight: float32 [2048, 3072], P('seq', 'grp')
Inputs may be any that keep to these rules, and one draw needn't show every extreme that they name: Clip c has 256 * clip_blocks[c] live video tokens at its start; some clip has all 4 blocks. Clip c has text_count[c] live text tokens at its start; some clip has all 256. Clip g * 4 + j goes to place j of group dest_group[g * 4 + j]. For a fixed j these groups all differ over g, and the 4 clips of one group go to different groups, so every group receives exactly 4 clips, one in each place.
All inputs are finite; a program needn't handle non-finite values.
Results may differ from a plain program's by a relative error of at most 0.023.
Values may be sent and summed in bfloat16 or wider, within the bound.
A program may use at most 256 MiB of HBM per device.

v0:
```python
import jax
import jax.numpy as jnp
from jax import lax
from jax.sharding import PartitionSpec as P

HEAD = 128
HEADS = 16
BLK = 256


NEG_FILL = -1e30


def pack_rows(selector, value_rows):
    flattened = value_rows.reshape(value_rows.shape[0], -1)
    return jnp.dot(selector, flattened, preferred_element_type=jnp.float32).astype(jnp.bfloat16)


def unpack_rows(selector, arrived, target_shape):
    gathered = jnp.dot(selector, arrived, preferred_element_type=jnp.float32).astype(jnp.bfloat16)
    return gathered.reshape(target_shape)


def attend(inputs):
    queries, key_rows, value_rows, live_query, live_key = inputs
    score_scale = HEAD ** (-0.5)
    scores = (
        jnp.einsum("qhe,khe->hqk", queries, key_rows, preferred_element_type=jnp.float32)
        * score_scale
    )
    scores = jnp.where(live_key[None, None, :], scores, NEG_FILL)
    row_max = jnp.max(scores, axis=-1, keepdims=True)
    exponent = jnp.exp(scores - row_max)
    weights = exponent / jnp.sum(exponent, axis=-1, keepdims=True)
    mixed = jnp.einsum(
        "hqk,khe->qhe", weights.astype(jnp.bfloat16), value_rows, preferred_element_type=jnp.float32
    )
    mixed = mixed * live_query[:, None, None].astype(jnp.float32)
    return (mixed.astype(jnp.bfloat16), weights)


def attend_back(inputs):
    queries, key_rows, value_rows, weights, grad_mixed = inputs
    score_scale = HEAD ** (-0.5)
    weights_b = weights.astype(jnp.bfloat16)
    grad_values = jnp.einsum(
        "hqk,qhe->khe", weights_b, grad_mixed, preferred_element_type=jnp.float32
    )
    grad_mix = jnp.einsum(
        "qhe,khe->hqk", grad_mixed, value_rows, preferred_element_type=jnp.float32
    )
    centre = jnp.sum(grad_mix * weights, axis=-1, keepdims=True)
    grad_scores = (weights * (grad_mix - centre) * score_scale).astype(jnp.bfloat16)
    grad_queries = jnp.einsum(
        "hqk,khe->qhe", grad_scores, key_rows, preferred_element_type=jnp.float32
    )
    grad_keys = jnp.einsum("hqk,qhe->khe", grad_scores, queries, preferred_element_type=jnp.float32)
    return (
        grad_queries.astype(jnp.bfloat16),
        grad_keys.astype(jnp.bfloat16),
        grad_values.astype(jnp.bfloat16),
    )


def on_device(qkv, text_kv, clip_blocks, text_count, dest_group, out_weight, grad_out):
    groups = lax.axis_size("grp")
    seat_count = lax.axis_size("seq")
    own_group = lax.axis_index("grp")
    own_seat = lax.axis_index("seq")
    per_group = qkv.shape[0]
    tok_dev = qkv.shape[1]
    txt_dev = text_kv.shape[1]
    clip_len = tok_dev * seat_count
    head_width = out_weight.shape[0]
    model_width = out_weight.shape[1]
    dest_table = dest_group.reshape(groups, per_group)
    own_dest = lax.dynamic_index_in_dim(dest_table, own_group, 0, keepdims=False)
    group_ids = jnp.arange(groups, dtype=jnp.int32)
    send_map = (own_dest[None, :] == group_ids[:, None]).astype(jnp.bfloat16)
    arrive = dest_table.T == own_group
    recv_map = arrive.astype(jnp.bfloat16)
    blocks_here = jnp.sum(jnp.where(arrive, clip_blocks.reshape(groups, per_group).T, 0), axis=1)
    count_here = jnp.sum(jnp.where(arrive, text_count.reshape(groups, per_group).T, 0), axis=1)
    video_shape = (per_group, tok_dev, 3, HEADS, HEAD)
    text_shape = (per_group, txt_dev, 2, HEADS, HEAD)
    moved_video, moved_text = (
        lax.all_to_all(pack_rows(send_map, qkv), "grp", split_axis=0, concat_axis=0, tiled=True),
        lax.all_to_all(
            pack_rows(send_map, text_kv), "grp", split_axis=0, concat_axis=0, tiled=True
        ),
    )
    video_here = unpack_rows(recv_map, moved_video, video_shape)
    text_here = unpack_rows(recv_map, moved_text, text_shape)
    video_heads, text_heads = (
        lax.all_to_all(video_here, "seq", split_axis=3, concat_axis=1, tiled=True),
        lax.all_to_all(text_here, "seq", split_axis=3, concat_axis=1, tiled=True),
    )
    txt_len = text_heads.shape[1]
    positions = jnp.arange(clip_len, dtype=jnp.int32)
    live_query = positions[None, :] < BLK * blocks_here[:, None]
    live_text = jnp.arange(txt_len, dtype=jnp.int32)[None, :] < count_here[:, None]
    live_key = jnp.concatenate([live_query, live_text], axis=1)
    queries = video_heads[:, :, 0]
    key_rows = jnp.concatenate([video_heads[:, :, 1], text_heads[:, :, 0]], axis=1)
    value_rows = jnp.concatenate([video_heads[:, :, 2], text_heads[:, :, 1]], axis=1)
    attended, weights = lax.map(attend, (queries, key_rows, value_rows, live_query, live_key))
    attended_tok = lax.all_to_all(attended, "seq", split_axis=1, concat_axis=2, tiled=True)
    attended_rows = attended_tok.reshape(per_group * tok_dev, head_width)
    output_rows = jnp.dot(attended_rows, out_weight, preferred_element_type=jnp.float32).astype(
        jnp.bfloat16
    )
    grad_rows = grad_out.reshape(per_group * tok_dev, model_width)
    own_positions = own_seat * tok_dev + jnp.arange(tok_dev, dtype=jnp.int32)
    live_rows = (
        (own_positions[None, :] < BLK * blocks_here[:, None]).reshape(-1, 1).astype(jnp.float32)
    )
    grad_att_rows = jnp.einsum(
        "td,rd->tr", grad_rows, out_weight, preferred_element_type=jnp.float32
    )
    grad_att_rows = (grad_att_rows * live_rows).astype(jnp.bfloat16)
    grad_attended = lax.all_to_all(
        grad_att_rows.reshape(per_group, tok_dev, HEADS, HEAD),
        "seq",
        split_axis=2,
        concat_axis=1,
        tiled=True,
    )
    partial_term = lax.psum_scatter(
        jnp.einsum(
            "tr,td->rd", attended_rows, grad_rows, preferred_element_type=jnp.float32
        ).astype(jnp.bfloat16),
        "seq",
        scatter_dimension=0,
        tiled=True,
    )
    grad_weight = lax.psum_scatter(partial_term, "grp", scatter_dimension=1, tiled=True).astype(
        jnp.float32
    ) / (per_group * groups)
    grad_queries, grad_keys, grad_values = lax.map(
        attend_back, (queries, key_rows, value_rows, weights, grad_attended)
    )
    grad_video = jnp.stack(
        [grad_queries, grad_keys[:, :clip_len], grad_values[:, :clip_len]], axis=2
    )
    grad_txt = jnp.stack([grad_keys[:, clip_len:], grad_values[:, clip_len:]], axis=2)
    back_video, back_text = (
        lax.all_to_all(grad_video, "seq", split_axis=1, concat_axis=3, tiled=True),
        lax.all_to_all(grad_txt, "seq", split_axis=1, concat_axis=3, tiled=True),
    )
    output_block = output_rows.reshape(per_group, tok_dev, model_width)
    grad_video_block = back_video.reshape(per_group, tok_dev, 3 * head_width)
    grad_text_block = back_text.reshape(per_group, txt_dev, 2 * head_width)
    return (output_block, grad_video_block, grad_text_block, grad_weight)


def solution(mesh):
    return jax.shard_map(
        on_device,
        mesh=mesh,
        in_specs=(
            P("grp", "seq", None),
            P("grp", "seq", None),
            P(),
            P(),
            P(),
            P(),
            P("grp", "seq", None),
        ),
        out_specs=(
            P("grp", "seq", None),
            P("grp", "seq", None),
            P("grp", "seq", None),
            P("seq", "grp"),
        ),
        check_vma=False,
    )
```

profile of v0, /device:TPU:27, one launch (start us, length us, event | category | flops | bytes accessed | tf_op | source)
XLA Modules:
  0.0 503.1 jit_solution(14621201836057250384)
XLA Ops:
  10.4 2.1 reduce.10
  12.5 3.1 reshape.195
  15.6 5.5 %all-to-all-start.2 = ((bf16[8,2,32768]{2,1,0:T(2,128)(2,1)}), bf16[8,2,32768]{2,1,0:T(2,128)(2,1)S(1)}, u32[]{:S(2)}, u32[]{:S(2)}) async-start(bf16[8,2,32768]{2,1,0:T(2,128)(2,1)} %reshape.195), calls=%async_computation.2 | async-start | bytes 2097152 | tf_op jit(solution)/shard_map/all_to_all | solution.py:88
  21.1 4.3 copy.153
  25.4 4.4 fusion.57
  29.8 9.1 %reduce.11 = bf16[8,393216]{1,0:T(8,128)(2,1)} reduce(bf16[8,1,393216]{2,0,1:T(8,128)(2,1)} %fusion.57, bf16[]{:T(256)} %broadcast.56), dimensions={1}, to_apply=%copy.114.reduce_sub_computation | reduce | bytes 12582914 | tf_op jit(solution)/shard_map/all_to_all | solution.py:87
  38.9 11.4 %reshape.197 = bf16[8,2,196608]{2,1,0:T(2,128)(2,1)} reshape(bf16[8,393216]{1,0:T(8,128)(2,1)} %reduce.11) | data formatting | bytes 12582912
  50.3 5.3 %all-to-all-start = ((bf16[8,2,196608]{2,1,0:T(2,128)(2,1)}), bf16[8,2,196608]{2,1,0:T(2,128)(2,1)}, u32[]{:S(2)}, u32[]{:S(2)}) async-start(bf16[8,2,196608]{2,1,0:T(2,128)(2,1)} %reshape.197), calls=%async_computation | async-start | bytes 12582912 | tf_op jit(solution)/shard_map/all_to_all | solution.py:87
  55.8 3.4 reshape.196
  59.2 2.9 fusion.66
  63.5 82.8 %all-to-all-done = bf16[8,2,196608]{2,1,0:T(2,128)(2,1)} async-done(((bf16[8,2,196608]{2,1,0:T(2,128)(2,1)}), bf16[8,2,196608]{2,1,0:T(2,128)(2,1)}, u32[]{:S(2)}, u32[]{:S(2)}) %all-to-all-start) | async-done | bytes 6291488 | tf_op jit(solution)/shard_map/all_to_all | solution.py:87
  146.3 10.3 %all-to-all-start.3 = ((bf16[4,16,2,16,128]{4,2,1,0,3:T(2,128)(2,1)}), bf16[4,16,2,16,128]{4,2,1,0,3:T(2,128)(2,1)S(1)}, u32[]{:S(2)}, u32[]{:S(2)}) async-start(bf16[4,16,2,16,128]{4,2,1,0,3:T(2,128)(2,1)} %copy.118), calls=%async_computation.3 | async-start | bytes 1048576 | tf_op jit(solution)/shard_map/all_to_all | solution.py:96
  156.6 11.0 %reshape.198 = bf16[8,1,393216]{2,1,0:T(2,128)(2,1)} reshape(bf16[8,2,196608]{2,1,0:T(2,128)(2,1)} %all-to-all-done) | data formatting | bytes 12582912
  167.6 12.3 %fusion.62 = bf16[1,4,3072,128]{3,1,2,0:T(4,128)(2,1)S(1)} fusion(pred[8,4]{1,0:T(8,128)(4,1)S(1)} %get-tuple-element.239, bf16[8,1,393216]{2,1,0:T(2,128)(2,1)} %reshape.198), kind=kOutput, calls=%fused_computation.67 | convolution fusion | flops 26738688 | bytes 9437216 | tf_op jit(solution)/shard_map/dot_general | solution.py:20
  180.3 2.5 copy.115
  182.8 7.2 %all-to-all-start.1 = ((bf16[4,64,3,16,128]{4,1,2,0,3:T(8,128)(2,1)}), bf16[4,64,3,16,128]{4,1,2,0,3:T(8,128)(2,1)}, u32[]{:S(2)}, u32[]{:S(2)}) async-start(bf16[4,64,3,16,128]{4,1,2,0,3:T(8,128)(2,1)} %copy.115), calls=%async_computation.1 | async-start | bytes 6291456 | tf_op jit(solution)/shard_map/all_to_all | solution.py:95
  190.4 42.4 %all-to-all-done.1 = bf16[4,64,3,16,128]{4,1,2,0,3:T(8,128)(2,1)} async-done(((bf16[4,64,3,16,128]{4,1,2,0,3:T(8,128)(2,1)}), bf16[4,64,3,16,128]{4,1,2,0,3:T(8,128)(2,1)}, u32[]{:S(2)}, u32[]{:S(2)}) %all-to-all-start.1) | async-done | bytes 3145760 | tf_op jit(solution)/shard_map/all_to_all | solution.py:95
  232.8 2.9 copy.116
  238.5 36.0 %while.26 = (s32[]{:T(128)}, bf16[4,1024,1,128]{1,3,2,0:T(8,128)(2,1)S(1)}, f32[4,1,1024,1280]{3,2,1,0:T(8,128)}, bf16[4,1280,1,128]{3,1,2,0:T(8,128)(2,1)}, pre...) while((s32[]{:T(128)}, ...), condition=%wide.region_5.6_spmd, body=%wide.region_2.5_spmd.sunk | while | flops 684456960 | bytes 27438436 | solution.py:106
  238.6 2.1 fusion.104
  241.7 3.0 bitcast_dynamic-update-slice_fusion.2
  244.7 2.8 fusion.106
  247.5 2.1 fusion.104
  250.7 3.0 bitcast_dynamic-update-slice_fusion.2
  253.7 2.8 fusion.106
  256.6 2.1 fusion.104
  259.7 3.1 bitcast_dynamic-update-slice_fusion.2
  262.8 2.8 fusion.106
  265.6 2.1 fusion.104
  268.7 3.0 bitcast_dynamic-update-slice_fusion.2
  271.7 2.8 fusion.106
  277.2 20.9 %all_to_all.123 = bf16[4,1024,1,128]{3,0,2,1:T(4,128)(2,1)S(1)} all-to-all(bf16[4,1024,1,128]{3,0,2,1:T(4,128)(2,1)S(1)} %copy.123), channel_id=1, replica_groups=mesh['grp'=8,'seq'=16] {'seq'}, dimensions={1} | all-to-all | bytes 2097152 | tf_op jit(solution)/shard_map/all_to_all | solution.py:107
  300.0 6.5 %convolution_convert_fusion.6 = bf16[2048,3072]{1,0:T(8,128)(2,1)} fusion(bf16[256,3072]{1,0:T(8,128)(2,1)S(1)} %bitcast.237, bf16[32,8,16,128]{3,2,1,0:T(8,128)(2,1)S(1)} %bitcast.242), kind=kOutput, calls=%fused_computation.60 | convolution fusion | flops 3227516928 | bytes 15204352 | tf_op jit(solution)/shard_map/tr,td->rd/dot_general | solution.py:129
  306.7 8.0 %fusion.65 = bf16[32,8,16,128]{3,1,2,0:T(8,128)(2,1)S(1)} fusion(bf16[256,3072]{1,0:T(8,128)(2,1)S(1)} %bitcast.236, bf16[2048,3072]{1,0:T(8,128)(2,1)} %param.16, f32[256]{0:T(256)S(1)} %reshape.191), kind=kOutput, calls=%fused_computation.68 | convolution fusion | flops 3222274048 | bytes 15205376 | tf_op jit(solution)/shard_map/td,rd->tr/dot_general | solution.py:117
  316.2 6.4 %all-to-all-start.5 = ((bf16[4,64,16,128]{3,1,0,2:T(8,128)(2,1)}), bf16[4,64,16,128]{3,1,0,2:T(8,128)(2,1)S(1)}, u32[]{:S(2)}, u32[]{:S(2)}) async-start(bf16[4,64,16,128]{3,1,0,2:T(8,128)(2,1)} %copy.126), calls=%async_computation.5 | async-start | bytes 2097152 | tf_op jit(solution)/shard_map/all_to_all | solution.py:121
  322.6 15.1 %all-to-all-done.5 = bf16[4,64,16,128]{3,1,0,2:T(8,128)(2,1)S(1)} async-done(((bf16[4,64,16,128]{3,1,0,2:T(8,128)(2,1)}), bf16[4,64,16,128]{3,1,0,2:T(8,128)(2,1)S(1)}, u32[]{:S(2)}, u32[]{:S(2)}) %all-to-all-start.5) | async-done | bytes 1048608 | tf_op jit(solution)/shard_map/all_to_all | solution.py:121
  338.8 70.2 %while.27 = (s32[]{:T(128)}, bf16[4,1024,1,128]{3,1,0,2:T(8,128)(2,1)}, bf16[4,1280,1,128]{3,1,0,2:T(8,128)(2,1)}, bf16[4,1280,1,128]{3,1,0,2:T(8,128)(2,1)}, bf...) while((s32[]{:T(128)}, ...), condition=%wide.region_8.9_spmd, body=%wide.region_6.8_spmd.sunk | while | flops 1350499328 | bytes 37499496 | solution.py:139
  338.8 3.6 fusion.113
  342.4 3.3 fusion.114
  347.5 3.1 fusion.116
  353.4 2.0 fusion.115
  356.2 3.6 fusion.113
  359.9 3.3 fusion.114
  364.9 3.2 fusion.116
  370.9 2.0 fusion.115
  373.7 3.8 fusion.113
  377.5 3.5 fusion.114
  382.8 3.1 fusion.116
  386.8 1.9 constant_dynamic-update-slice_fusion.6
  388.7 2.0 fusion.115
  391.6 3.6 fusion.113
  395.2 3.3 fusion.114
  400.2 3.1 fusion.116
  406.1 2.0 fusion.115
  412.5 7.5 %all-to-all-start.7 = ((bf16[4,256,2,1,128]{4,2,0,3,1:T(2,128)(2,1)}), bf16[4,256,2,1,128]{4,2,0,3,1:T(2,128)(2,1)S(1)}, u32[]{:S(2)}, u32[]{:S(2)}) async-start(bf16[4,256,2,1,128]{4,2,0,3,1:T(2,128)(2,1)} %copy.140), calls=%async_computation.7 | async-start | bytes 1048576 | tf_op jit(solution)/shard_map/all_to_all | solution.py:148
  421.6 4.1 copy.135
  425.7 4.9 all-to-all-done.7
  431.4 6.3 %all-to-all-start.6 = ((bf16[4,1024,3,1,128]{4,0,3,2,1:T(4,128)(2,1)}), bf16[4,1024,3,1,128]{4,0,3,2,1:T(4,128)(2,1)S(1)}, u32[]{:S(2)}, u32[]{:S(2)}) async-start(bf16[4,1024,3,1,128]{4,0,3,2,1:T(4,128)(2,1)} %copy.135), calls=%async_computation.6 | async-start | bytes 6291456 | tf_op jit(solution)/shard_map/all_to_all | solution.py:147
  437.8 2.3 copy.143
  442.2 2.1 reshape.189
  444.2 9.5 %convolution_convert_fusion.7 = bf16[256,3072]{1,0:T(8,128)(2,1)} fusion(bf16[2048,3072]{1,0:T(8,128)(2,1)} %param.16, bf16[32,8,16,128]{3,2,1,0:T(8,128)(2,1)} %bitcast.243), kind=kOutput, calls=%fused_computation.63 | convolution fusion | flops 3222011904 | bytes 15204352 | tf_op jit(solution)/shard_map/dot_general | solution.py:109
  453.7 30.8 %all-to-all-done.6 = bf16[4,1024,3,1,128]{4,0,3,2,1:T(4,128)(2,1)S(1)} async-done(((bf16[4,1024,3,1,128]{4,0,3,2,1:T(4,128)(2,1)}), bf16[4,1024,3,1,128]{4,0,3,2,1:T(4,128)(2,1)S(1)}, u32[]{:S(2)}, u32[]{:S(2)}) %all-to-all-start.6) | async-done | bytes 3145760 | tf_op jit(solution)/shard_map/all_to_all | solution.py:147
  485.0 3.7 copy.137
  488.7 5.6 %reshape.188 = bf16[4,64,6144]{2,1,0:T(8,128)(2,1)} reshape(bf16[4,64,3,16,1,128]{5,3,2,1,0,4:T(8,128)(2,1)} %copy.137) | data formatting | bytes 6291456 | tf_op jit(solution)/shard_map/reshape | solution.py:151
  (108 shorter events, 49.8 us)
Async XLA Ops:
  7.2 291.8 %copy-start = (bf16[4,64,3072]{2,1,0:T(8,128)(2,1)S(1)}, bf16[4,64,3072]{2,1,0:T(8,128)(2,1)}, u32[]{:S(2)}) copy-start(bf16[4,64,3072]{2,1,0:T(8,128)(2,1)} %param.17) | copy-start | bytes 4718596
  15.6 34.7 %all-to-all-start.2 = ((bf16[8,2,32768]{2,1,0:T(2,128)(2,1)}), bf16[8,2,32768]{2,1,0:T(2,128)(2,1)S(1)}, u32[]{:S(2)}, u32[]{:S(2)}) async-start(bf16[8,2,32768]{2,1,0:T(2,128)(2,1)} %reshape.195), calls=%async_computation.2 | async-start | bytes 2097152 | tf_op jit(solution)/shard_map/all_to_all | solution.py:88
  50.3 5.3 %copy-start.8 = (s32[32]{0:T(128)S(1)}, s32[32]{0:T(128)}, u32[]{:S(2)}) copy-start(s32[32]{0:T(128)} %param.13) | copy-start | bytes 388
  50.3 5.4 %copy-start.9 = (s32[32]{0:T(128)S(1)}, s32[32]{0:T(128)}, u32[]{:S(2)}) copy-start(s32[32]{0:T(128)} %param.14) | copy-start | bytes 388
  50.3 95.9 %all-to-all-start = ((bf16[8,2,196608]{2,1,0:T(2,128)(2,1)}), bf16[8,2,196608]{2,1,0:T(2,128)(2,1)}, u32[]{:S(2)}, u32[]{:S(2)}) async-start(bf16[8,2,196608]{2,1,0:T(2,128)(2,1)} %reshape.197), calls=%async_computation | async-start | bytes 12582912 | tf_op jit(solution)/shard_map/all_to_all | solution.py:87
  146.3 36.6 %all-to-all-start.3 = ((bf16[4,16,2,16,128]{4,2,1,0,3:T(2,128)(2,1)}), bf16[4,16,2,16,128]{4,2,1,0,3:T(2,128)(2,1)S(1)}, u32[]{:S(2)}, u32[]{:S(2)}) async-start(bf16[4,16,2,16,128]{4,2,1,0,3:T(2,128)(2,1)} %copy.118), calls=%async_computation.3 | async-start | bytes 1048576 | tf_op jit(solution)/shard_map/all_to_all | solution.py:96
  182.8 50.0 %all-to-all-start.1 = ((bf16[4,64,3,16,128]{4,1,2,0,3:T(8,128)(2,1)}), bf16[4,64,3,16,128]{4,1,2,0,3:T(8,128)(2,1)}, u32[]{:S(2)}, u32[]{:S(2)}) async-start(bf16[4,64,3,16,128]{4,1,2,0,3:T(8,128)(2,1)} %copy.115), calls=%async_computation.1 | async-start | bytes 6291456 | tf_op jit(solution)/shard_map/all_to_all | solution.py:95
  190.1 247.7 %reduce-scatter.5.cloned.1.call-start = ((), (), s32[]{:S(2)}) async-start(), calls=%async_computation.10 | async-start | bytes 13369344 | tf_op jit(solution)/shard_map/reduce_scatter | solution.py:128
  274.5 1.0 copy-start.6
  299.0 1.0 copy-start.2
  316.2 21.6 %all-to-all-start.5 = ((bf16[4,64,16,128]{3,1,0,2:T(8,128)(2,1)}), bf16[4,64,16,128]{3,1,0,2:T(8,128)(2,1)S(1)}, u32[]{:S(2)}, u32[]{:S(2)}) async-start(bf16[4,64,16,128]{3,1,0,2:T(8,128)(2,1)} %copy.126), calls=%async_computation.5 | async-start | bytes 2097152 | tf_op jit(solution)/shard_map/all_to_all | solution.py:121
  409.0 11.0 %copy-start.5 = (bf16[4,1280,1,128]{3,1,0,2:T(8,128)(2,1)S(1)}, bf16[4,1280,1,128]{3,1,0,2:T(8,128)(2,1)}, u32[]{:S(2)}) copy-start(bf16[4,1280,1,128]{3,1,0,2:T(8,128)(2,1)} %get-tuple-element.100) | copy-start | bytes 3932164
  409.0 11.1 %copy-start.4 = (bf16[4,1280,1,128]{3,1,0,2:T(8,128)(2,1)S(1)}, bf16[4,1280,1,128]{3,1,0,2:T(8,128)(2,1)}, u32[]{:S(2)}) copy-start(bf16[4,1280,1,128]{3,1,0,2:T(8,128)(2,1)} %get-tuple-element.99) | copy-start | bytes 3932164
  412.5 18.1 %all-to-all-start.7 = ((bf16[4,256,2,1,128]{4,2,0,3,1:T(2,128)(2,1)}), bf16[4,256,2,1,128]{4,2,0,3,1:T(2,128)(2,1)S(1)}, u32[]{:S(2)}, u32[]{:S(2)}) async-start(bf16[4,256,2,1,128]{4,2,0,3,1:T(2,128)(2,1)} %copy.140), calls=%async_computation.7 | async-start | bytes 1048576 | tf_op jit(solution)/shard_map/all_to_all | solution.py:148
  420.0 1.2 copy-start.7
  430.6 0.8 copy-start.3
  431.4 53.1 %all-to-all-start.6 = ((bf16[4,1024,3,1,128]{4,0,3,2,1:T(4,128)(2,1)}), bf16[4,1024,3,1,128]{4,0,3,2,1:T(4,128)(2,1)S(1)}, u32[]{:S(2)}, u32[]{:S(2)}) async-start(bf16[4,1024,3,1,128]{4,0,3,2,1:T(4,128)(2,1)} %copy.135), calls=%async_computation.6 | async-start | bytes 6291456 | tf_op jit(solution)/shard_map/all_to_all | solution.py:147
  437.7 56.6 %reduce-scatter.7.cloned.1.call-start = ((), (), s32[]{:S(2)}) async-start(), calls=%async_computation.11 | async-start | bytes 884736
  485.0 11.0 %copy-start.1 = (bf16[4,64,3072]{2,1,0:T(8,128)(2,1)S(1)}, bf16[4,64,3072]{2,1,0:T(8,128)(2,1)}, u32[]{:S(2)}) copy-start(bf16[4,64,3072]{2,1,0:T(8,128)(2,1)} %param.17) | copy-start | bytes 4718596
Sparse Core Ops, SparseCore 0:
  306.6 121.7 reduce-scatter.4
  441.1 36.3 reduce-scatter.6
where the time goes:
time: 512 us; the launch traced here: 503 us
  waiting for transfers between devices  176 us (34%)
  matrix products  105 us (21%)
  local copies, waits for them, and re-layouts  94.1 us (18%)
  starting transfers between devices  48.7 us (10%)
  other arithmetic  43.9 us (9%)
  blocking collectives  20.9 us (4%)
  between operations  14.6 us (3%)
    all_to_all x1, waiting for transfers between devices, on_device(): lax.all_to_all(pack_rows(send_map, qkv), 'grp', split_axis=0, concat_axis...  82.8 us
    unnamed x31, local copies, waits for them, and re-layouts  42.5 us
    all_to_all x1, waiting for transfers between devices, on_device(): lax.all_to_all(video_here, 'seq', split_axis=3, concat_axis=1, tiled=True)  42.4 us
    all_to_all x1, waiting for transfers between devices, on_device(): lax.all_to_all(grad_video, 'seq', split_axis=1, concat_axis=3, tiled=True)  30.8 us
    all_to_all x1, blocking collectives, on_device(): lax.all_to_all(attended, 'seq', split_axis=1, concat_axis=2, tiled=True)  20.9 us
    dot_general x2, matrix products, unpack_rows(): jnp.dot(selector, arrived, preferred_element_type=jnp.float32)  15.2 us
    all_to_all x1, waiting for transfers between devices, on_device(): lax.all_to_all(grad_att_rows.reshape(per_group, tok_dev, HEADS, HEAD), 's...  15.1 us
    dot_general x4, matrix products, attend_back(): jnp.einsum('qhe,khe->hqk', grad_mixed, value_rows, preferred_element_type...  14.7 us
  transfers between devices with their start and end apart: 9, of which 5 were waited for; matrix products, arithmetic and copies ran while one was open for 35% of the time, Pallas kernels for 0%

commit v1 on v0

v1 whole, which is shorter than its diff:
```python
import functools

import jax
import jax.numpy as jnp
from jax import lax
from jax.experimental import pallas as pl
from jax.experimental.pallas import tpu as pltpu
from jax.sharding import PartitionSpec as P

HEAD = 128
HEADS = 16
BLK = 256
GROUPS = 8
PLACES = 4
TOK = 64
TXT_DEV = 16
VIDEO = TOK * HEADS
TEXT = TXT_DEV * HEADS
KEYS = VIDEO + TEXT
HW = HEADS * HEAD
D = 3072
ROWS = 3 * TOK + 2 * TXT_DEV
SCALE = HEAD ** (-0.5)
LOG2E = 1.4426950408889634
NEG_FILL = -1e30
MESH = pl.DeviceIdType.MESH
BF = jnp.bfloat16
F32 = jnp.float32


def dot_nt(a, b):
    return lax.dot_general(a, b, (((1,), (1,)), ((), ())), preferred_element_type=F32)


def dot_nn(a, b):
    return lax.dot_general(a, b, (((1,), (0,)), ((), ())), preferred_element_type=F32)


def wait_for(ref, sem):
    pltpu.make_async_copy(ref, ref, sem).wait()


def source_group(dest_ref, group, place):
    found = jnp.int32(0)
    for g in range(GROUPS):
        found = jnp.where(dest_ref[g * PLACES + place] == group, g, found)
    return found


def relay_group(seat):
    return lax.rem(seat, 2) * 4 + lax.rem(seat // 2, 4)


def enter(others):
    barrier = pltpu.get_barrier_semaphore()
    g, s = lax.axis_index("grp"), lax.axis_index("seq")
    me = g * HEADS + s

    def greet(step, carry):
        other = lax.rem(me + step, GROUPS * HEADS)
        pl.semaphore_signal(
            barrier, inc=1, device_id=(other // HEADS, lax.rem(other, HEADS)), device_id_type=MESH
        )
        return carry

    lax.fori_loop(1, GROUPS * HEADS, greet, 0)
    pl.semaphore_wait(barrier, GROUPS * HEADS - 1)


def move_kernel(
    dest_ref, blocks_ref, qkv_ref, text_ref, grad_ref, weight_hbm,
    q_out, k_out, v_out, g_out,
    pack, relay0, relay1, relay2, relay3, sorted_, landed, weight, gpack, glanded,
    send1, recv1, send2, recv2, send3, recv3, wsem,
):
    g, s = lax.axis_index("grp"), lax.axis_index("seq")
    relays = (relay0, relay1, relay2, relay3)
    load = pltpu.make_async_copy(weight_hbm, weight, wsem)
    load.start()
    enter(None)
    relay = relay_group(s)
    half = s // 8
    home = relay == g

    for j in range(PLACES):
        def fill(h, carry):
            for t in range(3):
                pack[j, h, t * TOK:(t + 1) * TOK, :] = qkv_ref[
                    j, :, pl.ds(pl.multiple_of(t * HW + h * HEAD, HEAD), HEAD)
                ]
            for t in range(2):
                at = 3 * TOK + t * TXT_DEV
                pack[j, h, at:at + TXT_DEV, :] = text_ref[
                    j, :, pl.ds(pl.multiple_of(t * HW + h * HEAD, HEAD), HEAD)
                ]
            return carry

        lax.fori_loop(0, HEADS, fill, 0)

        def push(h):
            return pltpu.make_async_remote_copy(
                src_ref=pack.at[j, h], dst_ref=relays[j].at[g, half],
                send_sem=send1.at[j], recv_sem=recv1.at[j],
                device_id=(relay, h), device_id_type=MESH,
            )

        def spread(step, carry):
            push(lax.bitwise_xor(s, step)).start()
            return carry

        lax.fori_loop(1, HEADS, spread, 0)

        @pl.when(home)
        def _():
            pltpu.make_async_copy(pack.at[j, s], relays[j].at[g, half], recv1.at[j]).start()

        @pl.when(jnp.logical_not(home))
        def _():
            push(s).start()

    load.wait()
    grads = grad_ref[...].reshape(PLACES * TOK, D)
    live = []
    for j in range(PLACES):
        blocks = blocks_ref[source_group(dest_ref, g, j) * PLACES + j]
        live.append(jnp.where(s // 4 < blocks, 1.0, 0.0).astype(F32))

    def project(pair, carry):
        rows = pl.ds(pl.multiple_of(pair * 2 * HEAD, 2 * HEAD), 2 * HEAD)
        value = dot_nt(grads, weight[rows, :])
        for j in range(PLACES):
            part = (value[j * TOK:(j + 1) * TOK] * live[j]).astype(BF)
            gpack[2 * pair, j] = part[:, :HEAD]
            gpack[2 * pair + 1, j] = part[:, HEAD:]
        return carry

    lax.fori_loop(0, HEADS // 2, project, 0)

    def spread_g(step, carry):
        h = lax.bitwise_xor(s, step)
        pltpu.make_async_remote_copy(
            src_ref=gpack.at[h], dst_ref=glanded.at[s], send_sem=send3, recv_sem=recv3,
            device_id=(g, h), device_id_type=MESH,
        ).start()
        return carry

    lax.fori_loop(1, HEADS, spread_g, 0)
    glanded[s] = gpack[s]

    for j in range(PLACES):
        wait_for(relays[j], recv1.at[j])

        def regroup(step, carry):
            d = lax.bitwise_xor(g, step)
            came = source_group(dest_ref, d, j)
            sorted_[j, step] = relays[j][came]
            pltpu.make_async_remote_copy(
                src_ref=sorted_.at[j, step], dst_ref=landed.at[j, g],
                send_sem=send2.at[j], recv_sem=recv2.at[j],
                device_id=(d, s), device_id_type=MESH,
            ).start()
            return carry

        lax.fori_loop(1, GROUPS, regroup, 0)
        landed[j, g] = relays[j][source_group(dest_ref, g, j)]

    wait_for(glanded.at[pl.ds(1, HEADS - 1)], recv3)
    for r in range(HEADS):
        for j in range(PLACES):
            g_out[j, r * TOK:(r + 1) * TOK, :] = glanded[r, j]

    for j in range(PLACES):
        wait_for(landed.at[j, pl.ds(1, GROUPS - 1)], recv2.at[j])
        for r in range(HEADS):
            m, z = (r % 2) * 4 + (r // 2) % 4, r // 8
            q_out[j, r * TOK:(r + 1) * TOK, :] = landed[j, m, z, 0:TOK, :]
            k_out[j, r * TOK:(r + 1) * TOK, :] = landed[j, m, z, TOK:2 * TOK, :]
            v_out[j, r * TOK:(r + 1) * TOK, :] = landed[j, m, z, 2 * TOK:3 * TOK, :]
            lo = VIDEO + r * TXT_DEV
            k_out[j, lo:lo + TXT_DEV, :] = landed[j, m, z, 3 * TOK:3 * TOK + TXT_DEV, :]
            v_out[j, lo:lo + TXT_DEV, :] = landed[j, m, z, 3 * TOK + TXT_DEV:ROWS, :]

    for j in range(PLACES):
        @pl.when(home)
        def _():
            wait_for(pack.at[j, pl.ds(1, HEADS - 1)], send1.at[j])

        @pl.when(jnp.logical_not(home))
        def _():
            wait_for(pack.at[j], send1.at[j])

        wait_for(sorted_.at[j, pl.ds(1, GROUPS - 1)], send2.at[j])
    wait_for(gpack.at[pl.ds(1, HEADS - 1)], send3)


def move(dest_group, clip_blocks, qkv, text_kv, grad_out, out_weight):
    smem = pl.BlockSpec(memory_space=pltpu.SMEM)
    vmem = pl.BlockSpec(memory_space=pltpu.VMEM)
    relay = pltpu.VMEM((GROUPS, 2, ROWS, HEAD), BF)
    return pl.pallas_call(
        move_kernel,
        out_shape=(
            jax.ShapeDtypeStruct((PLACES, VIDEO, HEAD), BF),
            jax.ShapeDtypeStruct((PLACES, KEYS, HEAD), BF),
            jax.ShapeDtypeStruct((PLACES, KEYS, HEAD), BF),
            jax.ShapeDtypeStruct((PLACES, VIDEO, HEAD), BF),
        ),
        in_specs=[smem, smem, vmem, vmem, vmem, pl.BlockSpec(memory_space=pl.ANY)],
        out_specs=(vmem, vmem, vmem, vmem),
        scratch_shapes=[
            pltpu.VMEM((PLACES, HEADS, ROWS, HEAD), BF),
            relay, relay, relay, relay,
            pltpu.VMEM((PLACES, GROUPS, 2, ROWS, HEAD), BF),
            pltpu.VMEM((PLACES, GROUPS, 2, ROWS, HEAD), BF),
            pltpu.VMEM((HW, D), BF),
            pltpu.VMEM((HEADS, PLACES, TOK, HEAD), BF),
            pltpu.VMEM((HEADS, PLACES, TOK, HEAD), BF),
            pltpu.SemaphoreType.DMA((PLACES,)),
            pltpu.SemaphoreType.DMA((PLACES,)),
            pltpu.SemaphoreType.DMA((PLACES,)),
            pltpu.SemaphoreType.DMA((PLACES,)),
            pltpu.SemaphoreType.DMA,
            pltpu.SemaphoreType.DMA,
            pltpu.SemaphoreType.DMA,
        ],
        compiler_params=pltpu.CompilerParams(
            collective_id=0, has_side_effects=True, vmem_limit_bytes=56 * 1024 * 1024
        ),
        name="move",
    )(dest_group, clip_blocks, qkv, text_kv, grad_out, out_weight)


def attend_kernel(
    here_ref, q_ref, k_ref, v_ref, g_ref, o_ref, dq_ref, dk_ref, dv_ref, kt, vt, bias, dk_acc, dv_acc
):
    j = pl.program_id(0)
    blocks = here_ref[0, j]
    count = here_ref[1, j]
    kt[...] = k_ref[0].T
    vt[...] = v_ref[0].T
    row = lax.broadcasted_iota(jnp.int32, (KEYS, 2 * HEAD), 0)
    dead = jnp.logical_or(
        jnp.logical_and(row >= blocks * BLK, row < VIDEO), row >= VIDEO + count
    )
    bias[...] = jnp.where(dead, NEG_FILL, 0.0)
    dk_acc[...] = jnp.zeros_like(dk_acc)
    dv_acc[...] = jnp.zeros_like(dv_acc)

    def block(i, carry):
        at = pl.ds(pl.multiple_of(i * BLK, BLK), BLK)
        q = q_ref[0, at, :]
        g = g_ref[0, at, :]
        st = dot_nt(k_ref[0], q) + bias[...]
        top = jnp.max(st, axis=0, keepdims=True)
        e = jnp.exp2((st - top) * (SCALE * LOG2E))
        w = e * (1.0 / jnp.sum(e, axis=0, keepdims=True))
        wb = w.astype(BF)
        o_ref[0, at, :] = dot_nn(vt[...], wb).T.astype(BF)
        dv_acc[...] += dot_nn(wb, g)
        dp = dot_nt(v_ref[0], g)
        centre = jnp.sum(dp * w, axis=0, keepdims=True)
        ds = (w * (dp - centre) * SCALE).astype(BF)
        dq_ref[0, at, :] = dot_nn(kt[...], ds).T.astype(BF)
        dk_acc[...] += dot_nn(ds, q)
        return carry

    def blank(i, carry):
        at = pl.ds(pl.multiple_of(i * BLK, BLK), BLK)
        o_ref[0, at, :] = jnp.zeros((BLK, HEAD), BF)
        dq_ref[0, at, :] = jnp.zeros((BLK, HEAD), BF)
        return carry

    lax.fori_loop(0, blocks, block, 0)
    lax.fori_loop(blocks, VIDEO // BLK, blank, 0)
    dk_ref[0] = dk_acc[...].astype(BF)
    dv_ref[0] = dv_acc[...].astype(BF)


def attend(here, q, k, v, g):
    def spec(rows):
        return pl.BlockSpec((1, rows, HEAD), lambda j, here: (j, 0, 0))

    return pl.pallas_call(
        attend_kernel,
        out_shape=(
            jax.ShapeDtypeStruct((PLACES, VIDEO, HEAD), BF),
            jax.ShapeDtypeStruct((PLACES, VIDEO, HEAD), BF),
            jax.ShapeDtypeStruct((PLACES, KEYS, HEAD), BF),
            jax.ShapeDtypeStruct((PLACES, KEYS, HEAD), BF),
        ),
        grid_spec=pltpu.PrefetchScalarGridSpec(
            num_scalar_prefetch=1,
            grid=(PLACES,),
            in_specs=[spec(VIDEO), spec(KEYS), spec(KEYS), spec(VIDEO)],
            out_specs=(spec(VIDEO), spec(VIDEO), spec(KEYS), spec(KEYS)),
            scratch_shapes=[
                pltpu.VMEM((HEAD, KEYS), BF),
                pltpu.VMEM((HEAD, KEYS), BF),
                pltpu.VMEM((KEYS, 2 * HEAD), F32),
                pltpu.VMEM((KEYS, HEAD), F32),
                pltpu.VMEM((KEYS, HEAD), F32),
            ],
        ),
        compiler_params=pltpu.CompilerParams(vmem_limit_bytes=48 * 1024 * 1024),
        name="attend",
    )(here, q, k, v, g)


def on_device(qkv, text_kv, clip_blocks, text_count, dest_group, out_weight, grad_out):
    own_group = lax.axis_index("grp")
    arrive = dest_group.reshape(GROUPS, PLACES).T == own_group
    blocks_here = jnp.sum(jnp.where(arrive, clip_blocks.reshape(GROUPS, PLACES).T, 0), axis=1)
    count_here = jnp.sum(jnp.where(arrive, text_count.reshape(GROUPS, PLACES).T, 0), axis=1)
    here = jnp.stack([blocks_here, count_here])
    q, k, v, g = move(dest_group, clip_blocks, qkv, text_kv, grad_out, out_weight)
    attended, dq, dk, dv = attend(here, q, k, v, g)
    attended_tok = lax.all_to_all(
        attended[:, :, None, :], "seq", split_axis=1, concat_axis=2, tiled=True
    )
    attended_rows = attended_tok.reshape(PLACES * TOK, HW)
    out = jnp.dot(attended_rows, out_weight, preferred_element_type=F32).astype(BF)
    grad_rows = grad_out.reshape(PLACES * TOK, D)
    partial_term = lax.psum_scatter(
        jnp.einsum("tr,td->rd", attended_rows, grad_rows, preferred_element_type=F32).astype(BF),
        "seq", scatter_dimension=0, tiled=True,
    )
    grad_weight = lax.psum_scatter(partial_term, "grp", scatter_dimension=1, tiled=True).astype(
        F32
    ) / (PLACES * GROUPS)
    grad_video = jnp.stack([dq, dk[:, :VIDEO], dv[:, :VIDEO]], axis=2)[:, :, :, None, :]
    grad_txt = jnp.stack([dk[:, VIDEO:], dv[:, VIDEO:]], axis=2)[:, :, :, None, :]
    back_video = lax.all_to_all(grad_video, "seq", split_axis=1, concat_axis=3, tiled=True)
    back_text = lax.all_to_all(grad_txt, "seq", split_axis=1, concat_axis=3, tiled=True)
    return (
        out.reshape(PLACES, TOK, D),
        back_video.reshape(PLACES, TOK, 3 * HW),
        back_text.reshape(PLACES, TXT_DEV, 2 * HW),
        grad_weight,
    )


def solution(mesh):
    return jax.shard_map(
        on_device,
        mesh=mesh,
        in_specs=(
            P("grp", "seq", None),
            P("grp", "seq", None),
            P(),
            P(),
            P(),
            P(),
            P("grp", "seq", None),
        ),
        out_specs=(
            P("grp", "seq", None),
            P("grp", "seq", None),
            P("grp", "seq", None),
            P("seq", "grp"),
        ),
        check_vma=False,
    )
```

time: 512 us -> 377 us (0.74)
  the two profiles are of different devices: /device:TPU:27 before, /device:TPU:0 now
where the time goes in v1:
time: 377 us; the launch traced here: 376 us
  waiting for transfers between devices  148 us (39%)
  Pallas kernels  130 us (34%)
  local copies, waits for them, and re-layouts  30.4 us (8%)
  blocking collectives  27.9 us (7%)
  matrix products  16.1 us (4%)
  between operations  14.1 us (4%)
  starting transfers between devices  7.63 us (2%)
    reduce_scatter x1, waiting for transfers between devices, on_device(): lax.psum_scatter(jnp.einsum('tr,td->rd', attended_rows, grad_rows, prefer...  128 us
    pallas_call x1, Pallas kernels, move(): pl.pallas_call(move_kernel, out_shape=(jax.ShapeDtypeStruct((PLACES, VIDE...  111 us
    all_to_all x1, blocking collectives, on_device(): lax.all_to_all(attended[:, :, None, :], 'seq', split_axis=1, concat_axis=...  27.9 us
    pallas_call x1, Pallas kernels, attend(): pl.pallas_call(attend_kernel, out_shape=(jax.ShapeDtypeStruct((PLACES, VI...  18.8 us
    unnamed x3, waiting for transfers between devices  13.9 us
    dot_general x1, matrix products, on_device(): jnp.dot(attended_rows, out_weight, preferred_element_type=F32).astype(BF)  9.55 us
    unnamed x12, local copies, waits for them, and re-layouts  7.56 us
  transfers between devices with their start and end apart: 4, of which 3 were waited for; matrix products, arithmetic and copies ran while one was open for 9% of the time, Pallas kernels for 0%

profile of v1, /device:TPU:0, one launch (start us, length us, event | category | flops | bytes accessed | tf_op | source)
XLA Modules:
  0.0 376.3 jit_solution(8603791915575253941)
XLA Ops:
  7.2 0.0 reduce-scatter.5.cloned.1.call-start
  7.2 0.7 compare_select_fusion.1
  7.9 0.1 select_n.16
  8.0 0.1 select_n.18
  8.1 111.5 %move.1 = (bf16[4,1024,128]{2,1,0:T(8,128)(2,1)}, bf16[4,1280,128]{2,1,0:T(8,128)(2,1)}, bf16[4,1280,128]{2,1,0:T(8,128)(2,1)}, bf16[4,1024,128]{2,1,0:T(8,128)(2,1)}) custom-call(s32[32]{0:T(128)} %dest_ref.1, s32[32]{0:T(128)} %blocks_ref.1, bf16[4,64,6144]{2,1,0:T(8,128)(2,1)} %qkv_ref.1, bf16[4,16,4096]{2,1,0:T(8,128)(2,1)} %text_ref.1, ...), custom_call_target="tpu_custom_call" | custom-call | tf_op jit(solution)/shard_map/move/pallas_call | solution.py:200
  119.6 0.0 copy-start
  119.6 1.2 copy-done
  120.9 0.0 copy-start.1
  120.9 1.2 copy-done.1
  122.1 18.8 %attend.1 = (bf16[4,1024,128]{2,1,0:T(8,128)(2,1)S(1)}, bf16[4,1024,128]{2,1,0:T(8,128)(2,1)S(1)}, bf16[4,1280,128]{2,1,0:T(8,128)(2,1)S(1)}, bf16[4,1280,128]{2,1,0:T(8,128)(2,1)}) custom-call(s32[2,4]{1,0:T(2,128)S(1)} %pad_add_fusion.here_ref, bf16[4,1024,128]{2,1,0:T(8,128)(2,1)S(1)} %copy-done, bf16[4,1280,128]{2,1,0:T(8,128)(2,1)} %get-tuple-element.13.k_ref, ...), custom_call_target="tpu_custom_call" | custom-call | tf_op jit(solution)/shard_map/attend/pallas_call | solution.py:283
  140.9 0.0 copy-start.2
  140.9 0.8 copy.16
  141.7 27.9 %all_to_all.45 = bf16[4,1024,1,128]{3,0,2,1:T(4,128)(2,1)S(1)} all-to-all(bf16[4,1024,1,128]{3,0,2,1:T(4,128)(2,1)S(1)} %copy.16), channel_id=1, replica_groups=mesh['grp'=8,'seq'=16] {'seq'}, dimensions={1} | all-to-all | bytes 2097152 | tf_op jit(solution)/shard_map/all_to_all | solution.py:317
  169.6 0.7 copy.17
  170.3 0.0 copy-start.3
  170.3 1.0 copy-done.3
  171.3 0.0 copy-done.2
  171.3 6.5 %convolution_convert_fusion = bf16[2048,3072]{1,0:T(8,128)(2,1)} fusion(bf16[256,3072]{1,0:T(8,128)(2,1)S(1)} %bitcast.49, bf16[32,8,16,128]{3,2,1,0:T(8,128)(2,1)S(1)} %bitcast.50), kind=kOutput, calls=%fused_computation | convolution fusion | flops 3227516928 | bytes 15204352 | tf_op jit(solution)/shard_map/tr,td->rd/dot_general | solution.py:324
  177.8 0.0 reduce-scatter.5.cloned.1.call-update
  177.8 1.0 slice_bitcast_fusion.2
  178.8 0.1 maximum_bitcast_fusion.1
  178.9 1.2 copy.20
  180.1 3.6 all-to-all-start.2
  183.7 1.4 slice_bitcast_fusion
  185.1 0.3 maximum_bitcast_fusion
  185.4 4.1 %copy.18 = bf16[4,1024,3,1,128]{4,0,2,3,1:T(4,128)(2,1)} copy(bf16[4,1024,3,1,128]{4,1,0,2,3:T(8,128)(2,1)S(1)} %maximum_bitcast_fusion) | data formatting | bytes 6291456 | tf_op jit(solution)/shard_map/broadcast_in_dim | solution.py:330
  189.5 6.5 %all-to-all-done.2 = bf16[4,256,2,1,128]{4,0,2,3,1:T(4,128)(2,1)S(1)} async-done(((bf16[4,256,2,1,128]{4,0,2,3,1:T(4,128)(2,1)}), bf16[4,256,2,1,128]{4,0,2,3,1:T(4,128)(2,1)S(1)}, u32[]{:S(2)}, u32[]{:S(2)}) %all-to-all-start.2) | async-done | bytes 524320 | tf_op jit(solution)/shard_map/all_to_all | solution.py:333
  196.0 0.0 copy-start.4
  196.0 0.8 copy-done.4
  196.8 3.8 %all-to-all-start.1 = ((bf16[4,1024,3,1,128]{4,0,2,3,1:T(4,128)(2,1)}), bf16[4,1024,3,1,128]{4,0,2,3,1:T(4,128)(2,1)S(1)}, u32[]{:S(2)}, u32[]{:S(2)}) async-start(bf16[4,1024,3,1,128]{4,0,2,3,1:T(4,128)(2,1)} %copy.18), calls=%async_computation.1 | async-start | bytes 6291456 | tf_op jit(solution)/shard_map/all_to_all | solution.py:332
  200.6 0.2 reduce-scatter.7.cloned.1.call-start
  200.8 127.6 %reduce-scatter.5.cloned.1.call-done = bf16[128,3072]{1,0:T(8,128)(2,1)} async-done(((bf16[2048,3072]{1,0:T(8,128)(2,1)}), bf16[128,3072]{1,0:T(8,128)(2,1)}) %reduce-scatter.5.cloned.1.call-update) | async-done | bytes 786448 | tf_op jit(solution)/shard_map/reduce_scatter | solution.py:323
  328.5 2.3 copy.22
  330.8 0.0 reduce-scatter.7.cloned.1.call-update
  330.8 2.2 copy.21
  333.0 2.1 reshape.38
  335.0 9.6 %convolution_convert_fusion.1 = bf16[256,3072]{1,0:T(8,128)(2,1)} fusion(bf16[2048,3072]{1,0:T(8,128)(2,1)} %weight_hbm.1, bf16[32,8,16,128]{3,2,1,0:T(8,128)(2,1)} %bitcast.51), kind=kOutput, calls=%fused_computation.1 | convolution fusion | flops 3222011904 | bytes 15204352 | tf_op jit(solution)/shard_map/dot_general | solution.py:321
  344.6 0.0 all-to-all-done.1
  344.6 3.7 copy.19
  348.2 5.6 %reshape.37 = bf16[4,64,6144]{2,1,0:T(8,128)(2,1)} reshape(bf16[4,64,3,16,1,128]{5,3,2,1,0,4:T(8,128)(2,1)} %copy.19) | data formatting | bytes 6291456 | tf_op jit(solution)/shard_map/reshape | solution.py:336
  353.9 13.8 %reduce-scatter.7.cloned.1.call-done = bf16[384,128]{1,0:T(8,128)(2,1)} async-done(((bf16[3072,128]{1,0:T(8,128)(2,1)}), bf16[384,128]{1,0:T(8,128)(2,1)}) %reduce-scatter.7.cloned.1.call-update) | async-done | bytes 98320
  367.7 1.0 copy.23
  368.7 0.7 convert_multiply_fusion
  (3 shorter events, 0.1 us)
Async XLA Ops:
  7.2 321.3 %reduce-scatter.5.cloned.1.call-start = ((), (), s32[]{:S(2)}) async-start(), calls=%async_computation.5 | async-start | bytes 13369344 | tf_op jit(solution)/shard_map/reduce_scatter | solution.py:323
  119.6 1.2 copy-start
  120.9 1.2 copy-start.1
  140.9 30.4 %copy-start.2 = (bf16[4,64,3072]{2,1,0:T(8,128)(2,1)S(1)}, bf16[4,64,3072]{2,1,0:T(8,128)(2,1)}, u32[]{:S(2)}) copy-start(bf16[4,64,3072]{2,1,0:T(8,128)(2,1)} %grad_ref.1) | copy-start | bytes 4718596
  170.3 1.0 copy-start.3
  180.1 15.9 %all-to-all-start.2 = ((bf16[4,256,2,1,128]{4,0,2,3,1:T(4,128)(2,1)}), bf16[4,256,2,1,128]{4,0,2,3,1:T(4,128)(2,1)S(1)}, u32[]{:S(2)}, u32[]{:S(2)}) async-start(bf16[4,256,2,1,128]{4,0,2,3,1:T(4,128)(2,1)} %copy.20), calls=%async_computation.2 | async-start | bytes 1048576 | tf_op jit(solution)/shard_map/all_to_all | solution.py:333
  196.0 0.8 copy-start.4
  196.8 147.8 %all-to-all-start.1 = ((bf16[4,1024,3,1,128]{4,0,2,3,1:T(4,128)(2,1)}), bf16[4,1024,3,1,128]{4,0,2,3,1:T(4,128)(2,1)S(1)}, u32[]{:S(2)}, u32[]{:S(2)}) async-start(bf16[4,1024,3,1,128]{4,0,2,3,1:T(4,128)(2,1)} %copy.18), calls=%async_computation.1 | async-start | bytes 6291456 | tf_op jit(solution)/shard_map/all_to_all | solution.py:332
  200.6 167.1 %reduce-scatter.7.cloned.1.call-start = ((), (), s32[]{:S(2)}) async-start(), calls=%async_computation.6 | async-start | bytes 884736
Sparse Core Ops, SparseCore 0:
  178.0 150.4 reduce-scatter.4
  331.0 36.6 reduce-scatter.6

commit v2 on v1

--- a/solution.py
+++ b/solution.py
@@ -306,6 +306,295 @@
     )(here, q, k, v, g)
 
 
+def dot_tn(a, b):
+    return lax.dot_general(a, b, (((0,), (0,)), ((), ())), preferred_element_type=F32)
+
+
+X1, X2, Y1, Y2, Z1, Z2 = range(6)
+ORDERS = (
+    (X1, Y1, Z1, X2, Y2, Z2),
+    (Y1, Z1, X2, Y2, Z2, X1),
+    (Z1, X2, Y2, Z2, X1, Y1),
+    (X2, Y2, Z2, X1, Y1, Z1),
+    (Y2, Z2, X1, Y1, Z1, X2),
+    (Z2, X1, Y1, Z1, X2, Y2),
+)
+PARTS = 6
+CHIPS = 64
+EARLY = 8
+
+
+def ring_bits(u):
+    high = u // 2
+    return lax.bitwise_xor(lax.rem(u, 2), high), high
+
+
+def cube_bits(head_pair, column_block):
+    x1, x2 = ring_bits(lax.rem(head_pair, 4))
+    y1, y2 = ring_bits(lax.rem(column_block, 4))
+    z1, z2 = ring_bits(2 * (head_pair // 4) + column_block // 4)
+    return x1, x2, y1, y2, z1, z2
+
+
+def cube_index(bits, order, count=6):
+    at = jnp.int32(0)
+    for k in range(count):
+        at = at + bits[order[k]] * (CHIPS // 2 >> k)
+    return at
+
+
+def cube_neighbour(dim, g, s):
+    z_lo, y = g // 4, lax.rem(g, 4)
+    z_hi, x, core = s // 8, lax.rem(s // 2, 4), lax.rem(s, 2)
+    if dim == X1:
+        x = lax.bitwise_xor(x, 1)
+    if dim == X2:
+        x = 3 - x
+    if dim == Y1:
+        y = lax.bitwise_xor(y, 1)
+    if dim == Y2:
+        y = 3 - y
+    if dim in (Z1, Z2):
+        z_lo = 1 - z_lo
+    if dim == Z2:
+        z_hi = 1 - z_hi
+    return z_lo * 4 + y, (z_hi * 4 + x) * 2 + core
+
+
+def finish_kernel(
+    att_ref, dq_ref, dk_ref, dv_ref, grad_ref, weight_hbm,
+    out_ref, gq_ref, gt_ref, gw_ref,
+    alanded, afwd, gpart, pack, blanded, weight, acc, arrived, rows,
+    asend, arecv, fsend, frecv, gsend, grecv, bsend, brecv, rsend, rrecv, wsem,
+):
+    g, s = lax.axis_index("grp"), lax.axis_index("seq")
+    core = lax.rem(s, 2)
+    partner = lax.bitwise_xor(s, 1)
+    load = pltpu.make_async_copy(weight_hbm, weight, wsem)
+    load.start()
+
+    barrier = pltpu.get_barrier_semaphore()
+
+    def greet(step, carry):
+        pl.semaphore_signal(
+            barrier, inc=1, device_id=(g, lax.bitwise_xor(s, step)), device_id_type=MESH
+        )
+        return carry
+
+    lax.fori_loop(1, HEADS, greet, 0)
+    for dim in (Y1, Y2, Z1, Z2):
+        pl.semaphore_signal(
+            barrier, inc=1, device_id=cube_neighbour(dim, g, s), device_id_type=MESH
+        )
+    pl.semaphore_wait(barrier, HEADS - 1 + 4)
+
+    def token_rows(r):
+        return pl.ds(pl.multiple_of(r * TOK, TOK), TOK)
+
+    def text_rows(r):
+        return pl.ds(pl.multiple_of(VIDEO + r * TXT_DEV, TXT_DEV), TXT_DEV)
+
+    def send_att(step, carry):
+        r = lax.bitwise_xor(s, step)
+        pltpu.make_async_remote_copy(
+            src_ref=att_ref.at[:, token_rows(r), :], dst_ref=alanded.at[s],
+            send_sem=asend, recv_sem=arecv, device_id=(g, r), device_id_type=MESH,
+        ).start()
+        return carry
+
+    lax.fori_loop(1, HEADS, send_att, 0)
+    alanded[s] = att_ref[:, token_rows(s), :]
+    lend = pltpu.make_async_remote_copy(
+        src_ref=grad_ref, dst_ref=gpart, send_sem=gsend, recv_sem=grecv,
+        device_id=(g, partner), device_id_type=MESH,
+    )
+    lend.start()
+
+    def back(step):
+        r = lax.bitwise_xor(s, step)
+        return pltpu.make_async_remote_copy(
+            src_ref=pack.at[r], dst_ref=blanded.at[s],
+            send_sem=bsend, recv_sem=brecv.at[step], device_id=(g, r), device_id_type=MESH,
+        )
+
+    def send_back(step, carry):
+        r = lax.bitwise_xor(s, step)
+        for j in range(PLACES):
+            pack[r, j, 0:TOK, :] = dq_ref[j, token_rows(r), :]
+            pack[r, j, TOK:2 * TOK, :] = dk_ref[j, token_rows(r), :]
+            pack[r, j, 2 * TOK:3 * TOK, :] = dv_ref[j, token_rows(r), :]
+            pack[r, j, 3 * TOK:3 * TOK + TXT_DEV, :] = dk_ref[j, text_rows(r), :]
+            pack[r, j, 3 * TOK + TXT_DEV:ROWS, :] = dv_ref[j, text_rows(r), :]
+        back(step).start()
+        return carry
+
+    lax.fori_loop(1, EARLY, send_back, 0)
+
+    wait_for(alanded.at[pl.ds(1, HEADS - 1)], arecv)
+
+    def forward(i, carry):
+        pltpu.make_async_remote_copy(
+            src_ref=alanded.at[2 * i + 1 - core], dst_ref=afwd.at[i],
+            send_sem=fsend, recv_sem=frecv, device_id=(g, partner), device_id_type=MESH,
+        ).start()
+        return carry
+
+    lax.fori_loop(0, HEADS // 2, forward, 0)
+    for h in range(HEADS):
+        rows[:, h * HEAD:(h + 1) * HEAD] = alanded[h].reshape(PLACES * TOK, HEAD)
+    lend.wait_recv()
+    wait_for(afwd, frecv)
+
+    def term(pair, carry):
+        mine = jnp.concatenate(
+            [alanded[4 * pair + 2 * i + core].reshape(PLACES * TOK, HEAD) for i in range(2)], axis=1
+        )
+        theirs = jnp.concatenate(
+            [afwd[2 * pair + i].reshape(PLACES * TOK, HEAD) for i in range(2)], axis=1
+        )
+        both = jnp.concatenate([mine, theirs], axis=0)
+        for c in range(4):
+            columns = slice(c * 768, (c + 1) * 768)
+            right = jnp.concatenate(
+                [grad_ref[:, :, columns].reshape(PLACES * TOK, 768),
+                 gpart[:, :, columns].reshape(PLACES * TOK, 768)], axis=0)
+            value = dot_tn(both, right).astype(BF)
+            for i in range(2):
+                for b in range(2):
+                    bits = cube_bits(2 * pair + i, jnp.int32(2 * c + b))
+                    for p in range(PARTS):
+                        rh, ct = p // 3, p % 3
+                        top, left = i * HEAD + rh * 64, b * 384 + ct * HEAD
+                        acc[p, cube_index(bits, ORDERS[p])] = value[
+                            top:top + 64, left:left + HEAD
+                        ]
+        return carry
+
+    lax.fori_loop(0, 4, term, 0)
+
+    own = cube_bits(s // 2, g)
+
+    def exchange(p, k):
+        dim = ORDERS[p][k]
+        size = CHIPS // 2 >> k
+        start = cube_index(own, ORDERS[p], k) + (1 - own[dim]) * size
+        return pltpu.make_async_remote_copy(
+            src_ref=acc.at[p, pl.ds(start, size)],
+            dst_ref=arrived.at[p, pl.ds(CHIPS - 2 * size, size)],
+            send_sem=rsend.at[p, k], recv_sem=rrecv.at[p, k],
+            device_id=cube_neighbour(dim, g, s), device_id_type=MESH,
+        )
+
+    for p in range(PARTS):
+        exchange(p, 0).start()
+    lax.fori_loop(EARLY, HEADS, send_back, 0)
+
+    load.wait()
+
+    def project(c, carry):
+        columns = pl.ds(pl.multiple_of(c * 512, 512), 512)
+        value = dot_nn(rows[...], weight[:, columns]).astype(BF)
+        out_ref[:, :, columns] = value.reshape(PLACES, TOK, 512)
+        return carry
+
+    lax.fori_loop(0, D // 512, project, 0)
+
+    def place(h, block):
+        for j in range(PLACES):
+            for t in range(3):
+                gq_ref[j, :, pl.ds(pl.multiple_of(t * HW + h * HEAD, HEAD), HEAD)] = block[
+                    j, t * TOK:(t + 1) * TOK
+                ]
+            for t in range(2):
+                lo = 3 * TOK + t * TXT_DEV
+                gt_ref[j, :, pl.ds(pl.multiple_of(t * HW + h * HEAD, HEAD), HEAD)] = block[
+                    j, lo:lo + TXT_DEV
+                ]
+
+    for j in range(PLACES):
+        for t, ref in enumerate((dq_ref, dk_ref, dv_ref)):
+            gq_ref[j, :, pl.ds(pl.multiple_of(t * HW + s * HEAD, HEAD), HEAD)] = ref[
+                j, token_rows(s), :
+            ]
+        for t, ref in enumerate((dk_ref, dv_ref)):
+            gt_ref[j, :, pl.ds(pl.multiple_of(t * HW + s * HEAD, HEAD), HEAD)] = ref[
+                j, text_rows(s), :
+            ]
+
+    for k in range(6):
+        size = CHIPS // 2 >> k
+        for p in range(PARTS):
+            exchange(p, k).wait_recv()
+            start = cube_index(own, ORDERS[p], k + 1)
+
+            if k < 5:
+                chunk = min(size, 4)
+
+                def add(i, carry):
+                    at = pl.ds(start + i * chunk, chunk)
+                    come = pl.ds(CHIPS - 2 * size + i * chunk, chunk)
+                    acc[p, at] = (acc[p, at].astype(F32) + arrived[p, come].astype(F32)).astype(BF)
+                    return carry
+
+                lax.fori_loop(0, size // chunk, add, 0)
+                exchange(p, k + 1).start()
+            else:
+                rh, ct = p // 3, p % 3
+                total = acc[p, start].astype(F32) + arrived[p, CHIPS - 2].astype(F32)
+                gw_ref[rh * 64:(rh + 1) * 64, ct * HEAD:(ct + 1) * HEAD] = total * (
+                    1.0 / (PLACES * GROUPS)
+                )
+
+    def collect(step, carry):
+        back(step).wait_recv()
+        h = lax.bitwise_xor(s, step)
+        place(h, blanded[h])
+        return carry
+
+    lax.fori_loop(1, HEADS, collect, 0)
+
+    wait_for(alanded.at[pl.ds(1, HEADS - 1)], asend)
+    lend.wait_send()
+    wait_for(afwd, fsend)
+    wait_for(pack.at[pl.ds(1, HEADS - 1)], bsend)
+    for k in range(6):
+        for p in range(PARTS):
+            exchange(p, k).wait_send()
+
+
+def finish(attended, dq, dk, dv, grad_out, out_weight):
+    vmem = pl.BlockSpec(memory_space=pltpu.VMEM)
+    dma = pltpu.SemaphoreType.DMA
+    return pl.pallas_call(
+        finish_kernel,
+        out_shape=(
+            jax.ShapeDtypeStruct((PLACES, TOK, D), BF),
+            jax.ShapeDtypeStruct((PLACES, TOK, 3 * HW), BF),
+            jax.ShapeDtypeStruct((PLACES, TXT_DEV, 2 * HW), BF),
+            jax.ShapeDtypeStruct((HEAD, D // GROUPS), F32),
+        ),
+        in_specs=[vmem] * 5 + [pl.BlockSpec(memory_space=pl.ANY)],
+        out_specs=(vmem,) * 4,
+        scratch_shapes=[
+            pltpu.VMEM((HEADS, PLACES, TOK, HEAD), BF),
+            pltpu.VMEM((HEADS // 2, PLACES, TOK, HEAD), BF),
+            pltpu.VMEM((PLACES, TOK, D), BF),
+            pltpu.VMEM((HEADS, PLACES, ROWS, HEAD), BF),
+            pltpu.VMEM((HEADS, PLACES, ROWS, HEAD), BF),
+            pltpu.VMEM((HW, D), BF),
+            pltpu.VMEM((PARTS, CHIPS, 64, HEAD), BF),
+            pltpu.VMEM((PARTS, CHIPS, 64, HEAD), BF),
+            pltpu.VMEM((PLACES * TOK, HW), BF),
+            dma, dma, dma, dma, dma, dma, dma,
+            dma((HEADS,)), dma((PARTS, 6)), dma((PARTS, 6)), dma,
+        ],
+        compiler_params=pltpu.CompilerParams(
+            collective_id=1, has_side_effects=True, vmem_limit_bytes=60 * 1024 * 1024
+        ),
+        name="finish",
+    )(attended, dq, dk, dv, grad_out, out_weight)
+
+
 def on_device(qkv, text_kv, clip_blocks, text_count, dest_group, out_weight, grad_out):
     own_group = lax.axis_index("grp")
     arrive = dest_group.reshape(GROUPS, PLACES).T == own_group
@@ -314,29 +603,7 @@
     here = jnp.stack([blocks_here, count_here])
     q, k, v, g = move(dest_group, clip_blocks, qkv, text_kv, grad_out, out_weight)
     attended, dq, dk, dv = attend(here, q, k, v, g)
-    attended_tok = lax.all_to_all(
-        attended[:, :, None, :], "seq", split_axis=1, concat_axis=2, tiled=True
-    )
-    attended_rows = attended_tok.reshape(PLACES * TOK, HW)
-    out = jnp.dot(attended_rows, out_weight, preferred_element_type=F32).astype(BF)
-    grad_rows = grad_out.reshape(PLACES * TOK, D)
-    partial_term = lax.psum_scatter(
-        jnp.einsum("tr,td->rd", attended_rows, grad_rows, preferred_element_type=F32).astype(BF),
-        "seq", scatter_dimension=0, tiled=True,
-    )
-    grad_weight = lax.psum_scatter(partial_term, "grp", scatter_dimension=1, tiled=True).astype(
-        F32
-    ) / (PLACES * GROUPS)
-    grad_video = jnp.stack([dq, dk[:, :VIDEO], dv[:, :VIDEO]], axis=2)[:, :, :, None, :]
-    grad_txt = jnp.stack([dk[:, VIDEO:], dv[:, VIDEO:]], axis=2)[:, :, :, None, :]
-    back_video = lax.all_to_all(grad_video, "seq", split_axis=1, concat_axis=3, tiled=True)
-    back_text = lax.all_to_all(grad_txt, "seq", split_axis=1, concat_axis=3, tiled=True)
-    return (
-        out.reshape(PLACES, TOK, D),
-        back_video.reshape(PLACES, TOK, 3 * HW),
-        back_text.reshape(PLACES, TXT_DEV, 2 * HW),
-        grad_weight,
-    )
+    return finish(attended, dq, dk, dv, grad_out, out_weight)
 
 
 def solution(mesh):

time: 377 us -> 267 us (0.71)
  waiting for transfers between devices: 148 us -> 0 us
  Pallas kernels: 130 us -> 254 us
  blocking collectives: 27.9 us -> 0 us
  local copies, waits for them, and re-layouts: 30.4 us -> 11.6 us
  matrix products: 16.1 us -> 0 us
  between operations: 14.1 us -> 0.68 us
  starting transfers between devices: 7.63 us -> 0 us
    reduce_scatter x1 -> x0, waiting for transfers between devices: 128 us -> none  [on_device(): lax.psum_scatter(jnp.einsum('tr,td->rd', attended_rows, grad_rows, prefer...]
    pallas_call x0 -> x1, Pallas kernels: none -> 116 us  [finish(): pl.pallas_call(finish_kernel, out_shape=(jax.ShapeDtypeStruct((PLACES, TO...]
    all_to_all x1 -> x0, blocking collectives: 27.9 us -> none  [on_device(): lax.all_to_all(attended[:, :, None, :], 'seq', split_axis=1, concat_axis=...]
    dot_general x2 -> x0, matrix products: 16.1 us -> none  [the longest x1 9.55 us: on_device(): jnp.dot(attended_rows, out_weight, preferred_element_type=F32).astype(BF)]
    unnamed x3 -> x0, waiting for transfers between devices: 13.9 us -> none
    reshape x2 -> x0, local copies, waits for them, and re-layouts: 7.69 us -> none  [the longest x1 5.63 us: on_device(): back_video.reshape(PLACES, TOK, 3 * HW)]
    all_to_all x2 -> x0, starting transfers between devices: 7.37 us -> none  [the longest x1 3.8 us: on_device(): lax.all_to_all(grad_video, 'seq', split_axis=1, concat_axis=3, tiled=True)]
    pallas_call x1, Pallas kernels: 18.8 us -> 25.8 us  [attend(): pl.pallas_call(attend_kernel, out_shape=(jax.ShapeDtypeStruct((PLACES, VI...]
  transfers between devices with their start and end apart: 4 -> 0, of which waited for: 3 -> 0; matrix products, arithmetic and copies ran while one was open for 9% -> 0% of each run, Pallas kernels for 0% -> 0%
where the time goes in v2:
time: 267 us
  Pallas kernels  254 us (95%)
  local copies, waits for them, and re-layouts  11.6 us (4%)
    pallas_call x1, Pallas kernels, finish(): pl.pallas_call(finish_kernel, out_shape=(jax.ShapeDtypeStruct((PLACES, TO...  116 us
    pallas_call x1, Pallas kernels, move(): pl.pallas_call(move_kernel, out_shape=(jax.ShapeDtypeStruct((PLACES, VIDE...  111 us
    pallas_call x1, Pallas kernels, attend(): pl.pallas_call(attend_kernel, out_shape=(jax.ShapeDtypeStruct((PLACES, VI...  25.8 us
    unnamed x20, local copies, waits for them, and re-layouts  11.5 us

profile of v2, /device:TPU:0, one launch (start us, length us, event | category | flops | bytes accessed | tf_op | source)
XLA Modules:
  0.0 266.6 jit_solution(15854907148131802857)
XLA Ops:
  0.6 0.7 compare_select_fusion.1
  1.3 0.1 select_n.16
  1.4 0.1 select_n.18
  1.5 111.4 %move.1 = (bf16[4,1024,128]{2,1,0:T(8,128)(2,1)}, bf16[4,1280,128]{2,1,0:T(8,128)(2,1)}, bf16[4,1280,128]{2,1,0:T(8,128)(2,1)}, bf16[4,1024,128]{2,1,0:T(8,128)(2,1)}) custom-call(s32[32]{0:T(128)} %dest_ref.1, s32[32]{0:T(128)} %blocks_ref.1, bf16[4,64,6144]{2,1,0:T(8,128)(2,1)} %qkv_ref.1, bf16[4,16,4096]{2,1,0:T(8,128)(2,1)} %text_ref.1, ...), custom_call_target="tpu_custom_call" | custom-call | tf_op jit(solution)/shard_map/move/pallas_call | solution.py:200
  113.0 0.0 copy-start.3
  113.0 1.2 copy-done.3
  114.2 0.0 copy-start.4
  114.2 1.2 copy-done.4
  115.4 25.8 %attend.1 = (bf16[4,1024,128]{2,1,0:T(8,128)(2,1)S(1)}, bf16[4,1024,128]{2,1,0:T(8,128)(2,1)S(1)}, bf16[4,1280,128]{2,1,0:T(8,128)(2,1)S(1)}, bf16[4,1280,128]{2,1,0:T(8,128)(2,1)}) custom-call(s32[2,4]{1,0:T(2,128)S(1)} %pad_add_fusion.here_ref, bf16[4,1024,128]{2,1,0:T(8,128)(2,1)S(1)} %copy-done.3, bf16[4,1280,128]{2,1,0:T(8,128)(2,1)} %get-tuple-element.13.k_ref, ...), custom_call_target="tpu_custom_call" | custom-call | tf_op jit(solution)/shard_map/attend/pallas_call | solution.py:283
  141.2 0.0 copy-start
  141.2 1.1 copy-done
  142.3 0.0 copy-start.1
  142.3 1.0 copy-done.1
  143.3 0.0 copy-start.2
  143.3 1.0 copy-done.2
  144.3 116.3 %finish.1 = (bf16[4,64,3072]{2,1,0:T(8,128)(2,1)}, bf16[4,64,6144]{2,1,0:T(8,128)(2,1)}, bf16[4,16,4096]{2,1,0:T(8,128)(2,1)}, f32[128,384]{1,0:T(8,128)}) custom-call(bf16[4,1024,128]{2,1,0:T(8,128)(2,1)} %copy-done.1, bf16[4,1024,128]{2,1,0:T(8,128)(2,1)} %copy-done.2, bf16[4,1280,128]{2,1,0:T(8,128)(2,1)} %copy-done, ...), custom_call_target="tpu_custom_call" | custom-call | tf_op jit(solution)/shard_map/finish/pallas_call | solution.py:568
  260.6 0.0 copy-start.5
  260.6 2.8 %copy.15 = bf16[4,64,3072]{2,1,0:T(8,128)(2,1)} copy(bf16[4,64,3072]{2,1,0:T(8,128)(2,1)} %get-tuple-element.26) | data formatting | bytes 3145728
  263.4 0.0 copy-done.5
  263.4 0.0 copy-start.6
  263.4 0.0 copy-start.7
  263.4 1.7 copy.16
  265.1 0.0 copy-done.6
  265.1 0.8 copy.17
  265.9 0.0 copy-done.7
  265.9 0.7 copy.18
  (3 shorter events, 0.1 us)
Async XLA Ops:
  113.0 1.2 copy-start.3
  114.2 1.2 copy-start.4
  141.2 1.1 copy-start
  142.3 1.0 copy-start.1
  143.3 1.0 copy-start.2
  260.6 2.8 %copy-start.5 = (bf16[4,64,6144]{2,1,0:T(8,128)(2,1)S(1)}, bf16[4,64,6144]{2,1,0:T(8,128)(2,1)}, u32[]{:S(2)}) copy-start(bf16[4,64,6144]{2,1,0:T(8,128)(2,1)} %get-tuple-element.27) | copy-start | bytes 9437188
  263.4 1.7 copy-start.6
  263.4 2.5 copy-start.7

commit v3 on v1

v3 whole, which is shorter than its diff:
```python
import functools

import jax
import jax.numpy as jnp
from jax import lax
from jax.experimental import pallas as pl
from jax.experimental.pallas import tpu as pltpu
from jax.sharding import PartitionSpec as P

HEAD = 128
HEADS = 16
BLK = 256
GROUPS = 8
PLACES = 4
TOK = 64
TXT_DEV = 16
VIDEO = TOK * HEADS
TEXT = TXT_DEV * HEADS
KEYS = VIDEO + TEXT
HW = HEADS * HEAD
D = 3072
ROWS = 3 * TOK + 2 * TXT_DEV
SCALE = HEAD ** (-0.5)
LOG2E = 1.4426950408889634
NEG_FILL = -1e30
MESH = pl.DeviceIdType.MESH
BF = jnp.bfloat16
F32 = jnp.float32


def dot_nt(a, b):
    return lax.dot_general(a, b, (((1,), (1,)), ((), ())), preferred_element_type=F32)


def dot_nn(a, b):
    return lax.dot_general(a, b, (((1,), (0,)), ((), ())), preferred_element_type=F32)


def wait_for(ref, sem):
    pltpu.make_async_copy(ref, ref, sem).wait()


def source_group(dest_ref, group, place):
    found = jnp.int32(0)
    for g in range(GROUPS):
        found = jnp.where(dest_ref[g * PLACES + place] == group, g, found)
    return found


def relay_group(seat):
    return lax.rem(seat, 2) * 4 + lax.rem(seat // 2, 4)


def enter():
    barrier = pltpu.get_barrier_semaphore()
    g, s = lax.axis_index("grp"), lax.axis_index("seq")
    me = g * HEADS + s

    def greet(step, carry):
        other = lax.rem(me + step, GROUPS * HEADS)
        pl.semaphore_signal(
            barrier, inc=1, device_id=(other // HEADS, lax.rem(other, HEADS)), device_id_type=MESH
        )
        return carry

    lax.fori_loop(1, GROUPS * HEADS, greet, 0)
    pl.semaphore_wait(barrier, GROUPS * HEADS - 1)


def dot_tn(a, b):
    return lax.dot_general(a, b, (((0,), (0,)), ((), ())), preferred_element_type=F32)


X1, X2, Y1, Y2, Z1, Z2 = range(6)
ORDERS = (
    (X1, Y1, Z1, X2, Y2, Z2),
    (Y1, Z1, X2, Y2, Z2, X1),
    (Z1, X2, Y2, Z2, X1, Y1),
    (X2, Y2, Z2, X1, Y1, Z1),
    (Y2, Z2, X1, Y1, Z1, X2),
    (Z2, X1, Y1, Z1, X2, Y2),
)
PARTS = 6
CHIPS = 64
COLUMNS = 512


def ring_bits(u):
    high = u // 2
    return lax.bitwise_xor(lax.rem(u, 2), high), high


def cube_bits(head_pair, column_block):
    x1, x2 = ring_bits(lax.rem(head_pair, 4))
    y1, y2 = ring_bits(lax.rem(column_block, 4))
    z1, z2 = ring_bits(2 * (head_pair // 4) + column_block // 4)
    return x1, x2, y1, y2, z1, z2


def cube_index(bits, order, count=6):
    at = jnp.int32(0)
    for k in range(count):
        at = at + bits[order[k]] * (CHIPS // 2 >> k)
    return at


def cube_neighbour(dim, g, s):
    z_lo, y = g // 4, lax.rem(g, 4)
    z_hi, x, core = s // 8, lax.rem(s // 2, 4), lax.rem(s, 2)
    if dim == X1:
        x = lax.bitwise_xor(x, 1)
    if dim == X2:
        x = 3 - x
    if dim == Y1:
        y = lax.bitwise_xor(y, 1)
    if dim == Y2:
        y = 3 - y
    if dim in (Z1, Z2):
        z_lo = 1 - z_lo
    if dim == Z2:
        z_hi = 1 - z_hi
    return z_lo * 4 + y, (z_hi * 4 + x) * 2 + core


def kernel(
    dest_ref, blocks_ref, count_ref, qkv_hbm, text_hbm, grad_hbm, weight_hbm,
    out_ref, gq_ref, gt_ref, gw_ref,
    pack, relay0, relay1, relay2, relay3, sorted_, landed, gpack, glanded,
    wide, total, q_s, k_s, v_s, g_s, kt, vt, bias, o_s, dq_s, dk_s, dv_s,
    alanded, afwd, gpart, blanded, acc, arrived, rows,
    load_sem, wide_sem, send1, recv1, send2, recv2, send3, recv3,
    asend, arecv, fsend, frecv, lend_send, lend_recv, bsend, brecv, rsend, rrecv,
):
    g, s = lax.axis_index("grp"), lax.axis_index("seq")
    core = lax.rem(s, 2)
    partner = lax.bitwise_xor(s, 1)
    relays = (relay0, relay1, relay2, relay3)
    relay = relay_group(s)
    half = s // 8
    home = relay == g
    away = jnp.logical_not(home)

    def head_columns(t, h):
        return pl.ds(pl.multiple_of(t * HW + h * HEAD, HEAD), HEAD)

    def token_rows(r):
        return pl.ds(pl.multiple_of(r * TOK, TOK), TOK)

    def text_rows(r):
        return pl.ds(pl.multiple_of(VIDEO + r * TXT_DEV, TXT_DEV), TXT_DEV)

    loads = [pltpu.make_async_copy(qkv_hbm.at[j], gq_ref.at[j], load_sem.at[j]) for j in range(PLACES)]
    loads.append(pltpu.make_async_copy(text_hbm, gt_ref, load_sem.at[PLACES]))
    loads.append(pltpu.make_async_copy(grad_hbm, out_ref, load_sem.at[PLACES + 1]))

    def widen(c):
        return pltpu.make_async_copy(
            weight_hbm.at[:, c * COLUMNS:(c + 1) * COLUMNS], wide.at[c % 2], wide_sem.at[c % 2]
        )

    for load in loads:
        load.start()
    widen(0).start()
    widen(1).start()
    enter()

    def push(j, h):
        return pltpu.make_async_remote_copy(
            src_ref=pack.at[j, h], dst_ref=relays[j].at[g, half],
            send_sem=send1.at[j], recv_sem=recv1.at[j],
            device_id=(relay, h), device_id_type=MESH,
        )

    def spread(j):
        loads[j].wait()

        def one(step, carry):
            h = lax.bitwise_xor(s, step)
            for t in range(3):
                pack[j, h, t * TOK:(t + 1) * TOK, :] = gq_ref[j, :, head_columns(t, h)]
            for t in range(2):
                at = 3 * TOK + t * TXT_DEV
                pack[j, h, at:at + TXT_DEV, :] = gt_ref[j, :, head_columns(t, h)]

            @pl.when(jnp.logical_or(step > 0, away))
            def _():
                push(j, h).start()

            return carry

        lax.fori_loop(0, HEADS, one, 0)

        @pl.when(home)
        def _():
            pltpu.make_async_copy(pack.at[j, s], relays[j].at[g, half], recv1.at[j]).start()

    def spread_done(j):
        @pl.when(home)
        def _():
            wait_for(pack.at[j, pl.ds(1, HEADS - 1)], send1.at[j])

        @pl.when(away)
        def _():
            wait_for(pack.at[j], send1.at[j])

    def regroup(j):
        wait_for(relays[j], recv1.at[j])
        if j >= 2:
            wait_for(sorted_.at[j % 2, pl.ds(1, GROUPS - 1)], send2.at[j - 2])

        def one(step, carry):
            d = lax.bitwise_xor(g, step)
            sorted_[j % 2, step] = relays[j][source_group(dest_ref, d, j)]
            pltpu.make_async_remote_copy(
                src_ref=sorted_.at[j % 2, step], dst_ref=landed.at[j, g],
                send_sem=send2.at[j], recv_sem=recv2.at[j],
                device_id=(d, s), device_id_type=MESH,
            ).start()
            return carry

        lax.fori_loop(1, GROUPS, one, 0)
        landed[j, g] = relays[j][source_group(dest_ref, g, j)]

    def project_grads():
        for c in range(D // COLUMNS):
            widen(c).wait()
            part = dot_nt(
                out_ref[:, :, c * COLUMNS:(c + 1) * COLUMNS].reshape(PLACES * TOK, COLUMNS),
                wide[c % 2],
            )
            total[...] = part if c == 0 else total[...] + part
            widen((c + 2) % (D // COLUMNS)).start()
        for j in range(PLACES):
            blocks = blocks_ref[source_group(dest_ref, g, j) * PLACES + j]
            live = jnp.where(s // 4 < blocks, 1.0, 0.0).astype(F32)
            for h in range(HEADS):
                gpack[h, j] = (
                    total[j * TOK:(j + 1) * TOK, h * HEAD:(h + 1) * HEAD] * live
                ).astype(BF)

        def one(step, carry):
            h = lax.bitwise_xor(s, step)
            pltpu.make_async_remote_copy(
                src_ref=gpack.at[h], dst_ref=glanded.at[s], send_sem=send3, recv_sem=recv3,
                device_id=(g, h), device_id_type=MESH,
            ).start()
            return carry

        lax.fori_loop(1, HEADS, one, 0)
        glanded[s] = gpack[s]

    def attend(j):
        wait_for(landed.at[j, pl.ds(1, GROUPS - 1)], recv2.at[j])
        for r in range(HEADS):
            m, z = (r % 2) * 4 + (r // 2) % 4, r // 8
            here = slice(r * TOK, (r + 1) * TOK)
            text = slice(VIDEO + r * TXT_DEV, VIDEO + (r + 1) * TXT_DEV)
            q_s[here, :] = landed[j, m, z, 0:TOK, :]
            k_s[here, :] = landed[j, m, z, TOK:2 * TOK, :]
            v_s[here, :] = landed[j, m, z, 2 * TOK:3 * TOK, :]
            k_s[text, :] = landed[j, m, z, 3 * TOK:3 * TOK + TXT_DEV, :]
            v_s[text, :] = landed[j, m, z, 3 * TOK + TXT_DEV:ROWS, :]
            g_s[here, :] = glanded[r, j]
        clip = source_group(dest_ref, g, j) * PLACES + j
        blocks = blocks_ref[clip]
        count = count_ref[clip]
        kt[...] = k_s[...].T
        vt[...] = v_s[...].T
        row = lax.broadcasted_iota(jnp.int32, (KEYS, HEAD), 0)
        dead = jnp.logical_or(
            jnp.logical_and(row >= blocks * BLK, row < VIDEO), row >= VIDEO + count
        )
        bias[...] = jnp.where(dead, NEG_FILL, 0.0)
        dk_s[...] = jnp.zeros_like(dk_s)
        dv_s[...] = jnp.zeros_like(dv_s)

        def one(i, carry):
            at = pl.ds(pl.multiple_of(i * BLK, BLK), BLK)
            q = q_s[at, :]
            gr = g_s[at, :]
            live = jnp.where(i < blocks, 1.0, 0.0).astype(F32)
            st = dot_nt(k_s[...], q) + jnp.concatenate([bias[...], bias[...]], axis=1)
            top = jnp.max(st, axis=0, keepdims=True)
            e = jnp.exp2((st - top) * (SCALE * LOG2E))
            w = e * (1.0 / jnp.sum(e, axis=0, keepdims=True))
            wb = w.astype(BF)
            o_s[j, at, :] = (dot_nn(vt[...], wb) * live).T.astype(BF)
            dv_s[...] += dot_nn(wb, gr)
            dp = dot_nt(v_s[...], gr)
            centre = jnp.sum(dp * w, axis=0, keepdims=True)
            ds = (w * (dp - centre) * SCALE).astype(BF)
            dq_s[at, :] = dot_nn(kt[...], ds).T.astype(BF)
            dk_s[...] += dot_nn(ds, q)
            return carry

        lax.fori_loop(0, VIDEO // BLK, one, 0)

        def send_att(step, carry):
            r = lax.bitwise_xor(s, step)
            pltpu.make_async_remote_copy(
                src_ref=o_s.at[j, token_rows(r), :], dst_ref=alanded.at[s, j],
                send_sem=asend.at[j], recv_sem=arecv.at[j], device_id=(g, r), device_id_type=MESH,
            ).start()
            return carry

        lax.fori_loop(1, HEADS, send_att, 0)
        alanded[s, j] = o_s[j, token_rows(s), :]
        spread_done(j)

        def send_back(step, carry):
            r = lax.bitwise_xor(s, step)
            pack[j, r, 0:TOK, :] = dq_s[token_rows(r), :]
            pack[j, r, TOK:2 * TOK, :] = dk_s[token_rows(r), :].astype(BF)
            pack[j, r, 2 * TOK:3 * TOK, :] = dv_s[token_rows(r), :].astype(BF)
            pack[j, r, 3 * TOK:3 * TOK + TXT_DEV, :] = dk_s[text_rows(r), :].astype(BF)
            pack[j, r, 3 * TOK + TXT_DEV:ROWS, :] = dv_s[text_rows(r), :].astype(BF)

            @pl.when(step > 0)
            def _():
                pltpu.make_async_remote_copy(
                    src_ref=pack.at[j, r], dst_ref=blanded.at[j, s],
                    send_sem=bsend.at[j], recv_sem=brecv.at[j],
                    device_id=(g, r), device_id_type=MESH,
                ).start()

            return carry

        lax.fori_loop(0, HEADS, send_back, 0)
        blanded[j, s] = pack[j, s]

    def forward(j):
        wait_for(alanded.at[pl.ds(1, HEADS - 1), j], arecv.at[j])

        def one(i, carry):
            pltpu.make_async_remote_copy(
                src_ref=alanded.at[2 * i + 1 - core, j], dst_ref=afwd.at[i, j],
                send_sem=fsend.at[j], recv_sem=frecv.at[j],
                device_id=(g, partner), device_id_type=MESH,
            ).start()
            return carry

        lax.fori_loop(0, HEADS // 2, one, 0)
        for h in range(HEADS):
            rows[j * TOK:(j + 1) * TOK, h * HEAD:(h + 1) * HEAD] = alanded[h, j]

    def collect(j):
        wait_for(blanded.at[j, pl.ds(1, HEADS - 1)], brecv.at[j])

        def one(h, carry):
            for t in range(3):
                gq_ref[j, :, head_columns(t, h)] = blanded[j, h, t * TOK:(t + 1) * TOK, :]
            for t in range(2):
                at = 3 * TOK + t * TXT_DEV
                gt_ref[j, :, head_columns(t, h)] = blanded[j, h, at:at + TXT_DEV, :]
            return carry

        lax.fori_loop(0, HEADS, one, 0)

    def term(pair, carry):
        mine = jnp.concatenate(
            [alanded[4 * pair + 2 * i + core].reshape(PLACES * TOK, HEAD) for i in range(2)], axis=1
        )
        theirs = jnp.concatenate(
            [afwd[2 * pair + i].reshape(PLACES * TOK, HEAD) for i in range(2)], axis=1
        )
        both = jnp.concatenate([mine, theirs], axis=0)
        for c in range(4):
            columns = slice(c * 768, (c + 1) * 768)
            right = jnp.concatenate(
                [out_ref[:, :, columns].reshape(PLACES * TOK, 768),
                 gpart[:, :, columns].reshape(PLACES * TOK, 768)], axis=0)
            value = dot_tn(both, right).astype(BF)
            for i in range(2):
                for b in range(2):
                    bits = cube_bits(2 * pair + i, jnp.int32(2 * c + b))
                    for p in range(PARTS):
                        rh, ct = p // 3, p % 3
                        top, left = i * HEAD + rh * 64, b * 384 + ct * HEAD
                        acc[p, cube_index(bits, ORDERS[p])] = value[
                            top:top + 64, left:left + HEAD
                        ]
        return carry

    own = cube_bits(s // 2, g)

    def exchange(p, k):
        dim = ORDERS[p][k]
        size = CHIPS // 2 >> k
        start = cube_index(own, ORDERS[p], k) + (1 - own[dim]) * size
        return pltpu.make_async_remote_copy(
            src_ref=acc.at[p, pl.ds(start, size)],
            dst_ref=arrived.at[p, pl.ds(CHIPS - 2 * size, size)],
            send_sem=rsend.at[p, k], recv_sem=rrecv.at[p, k],
            device_id=cube_neighbour(dim, g, s), device_id_type=MESH,
        )

    def reduce_stage(k):
        size = CHIPS // 2 >> k
        for p in range(PARTS):
            exchange(p, k).wait_recv()
            start = cube_index(own, ORDERS[p], k + 1)
            if k < 5:
                chunk = min(size, 4)

                def add(i, carry):
                    at = pl.ds(start + i * chunk, chunk)
                    come = pl.ds(CHIPS - 2 * size + i * chunk, chunk)
                    acc[p, at] = (acc[p, at].astype(F32) + arrived[p, come].astype(F32)).astype(BF)
                    return carry

                lax.fori_loop(0, size // chunk, add, 0)
                exchange(p, k + 1).start()
            else:
                rh, ct = p // 3, p % 3
                value = acc[p, start].astype(F32) + arrived[p, CHIPS - 2].astype(F32)
                gw_ref[rh * 64:(rh + 1) * 64, ct * HEAD:(ct + 1) * HEAD] = value * (
                    1.0 / (PLACES * GROUPS)
                )

    loads[PLACES].wait()
    spread(0)
    spread(1)
    loads[PLACES + 1].wait()
    lend = pltpu.make_async_remote_copy(
        src_ref=out_ref, dst_ref=gpart, send_sem=lend_send, recv_sem=lend_recv,
        device_id=(g, partner), device_id_type=MESH,
    )
    lend.start()
    project_grads()
    regroup(0)
    spread(2)
    regroup(1)
    spread(3)
    wait_for(glanded.at[pl.ds(1, HEADS - 1)], recv3)
    attend(0)
    regroup(2)
    attend(1)
    regroup(3)
    forward(0)
    attend(2)
    forward(1)
    attend(3)
    forward(2)
    collect(0)
    lend.wait()
    forward(3)
    for j in range(PLACES):
        wait_for(afwd.at[:, j], frecv.at[j])
    lax.fori_loop(0, 4, term, 0)
    for p in range(PARTS):
        exchange(p, 0).start()
    for c in range(D // COLUMNS):
        widen(c).wait()
        value = dot_nn(rows[...], wide[c % 2]).astype(BF)
        out_ref[:, :, c * COLUMNS:(c + 1) * COLUMNS] = value.reshape(PLACES, TOK, COLUMNS)
        if c + 2 < D // COLUMNS:
            widen(c + 2).start()
    collect(1)
    collect(2)
    for k in range(6):
        reduce_stage(k)
    collect(3)

    for j in range(PLACES):
        if j >= 2:
            wait_for(sorted_.at[j % 2, pl.ds(1, GROUPS - 1)], send2.at[j])
        wait_for(o_s.at[j, pl.ds(TOK, VIDEO - TOK)], asend.at[j])
        wait_for(afwd.at[:, j], fsend.at[j])
        wait_for(pack.at[j, pl.ds(1, HEADS - 1)], bsend.at[j])
    wait_for(gpack.at[pl.ds(1, HEADS - 1)], send3)
    for k in range(6):
        for p in range(PARTS):
            exchange(p, k).wait_send()


def on_device(qkv, text_kv, clip_blocks, text_count, dest_group, out_weight, grad_out):
    smem = pl.BlockSpec(memory_space=pltpu.SMEM)
    vmem = pl.BlockSpec(memory_space=pltpu.VMEM)
    hbm = pl.BlockSpec(memory_space=pl.ANY)
    dma = pltpu.SemaphoreType.DMA
    relay = pltpu.VMEM((GROUPS, 2, ROWS, HEAD), BF)
    return pl.pallas_call(
        kernel,
        out_shape=(
            jax.ShapeDtypeStruct((PLACES, TOK, D), BF),
            jax.ShapeDtypeStruct((PLACES, TOK, 3 * HW), BF),
            jax.ShapeDtypeStruct((PLACES, TXT_DEV, 2 * HW), BF),
            jax.ShapeDtypeStruct((HEAD, D // GROUPS), F32),
        ),
        in_specs=[smem] * 3 + [hbm] * 4,
        out_specs=(vmem,) * 4,
        scratch_shapes=[
            pltpu.VMEM((PLACES, HEADS, ROWS, HEAD), BF),
            relay, relay, relay, relay,
            pltpu.VMEM((2, GROUPS, 2, ROWS, HEAD), BF),
            pltpu.VMEM((PLACES, GROUPS, 2, ROWS, HEAD), BF),
            pltpu.VMEM((HEADS, PLACES, TOK, HEAD), BF),
            pltpu.VMEM((HEADS, PLACES, TOK, HEAD), BF),
            pltpu.VMEM((2, HW, COLUMNS), BF),
            pltpu.VMEM((PLACES * TOK, HW), F32),
            pltpu.VMEM((VIDEO, HEAD), BF),
            pltpu.VMEM((KEYS, HEAD), BF),
            pltpu.VMEM((KEYS, HEAD), BF),
            pltpu.VMEM((VIDEO, HEAD), BF),
            pltpu.VMEM((HEAD, KEYS), BF),
            pltpu.VMEM((HEAD, KEYS), BF),
            pltpu.VMEM((KEYS, HEAD), F32),
            pltpu.VMEM((PLACES, VIDEO, HEAD), BF),
            pltpu.VMEM((VIDEO, HEAD), BF),
            pltpu.VMEM((KEYS, HEAD), F32),
            pltpu.VMEM((KEYS, HEAD), F32),
            pltpu.VMEM((HEADS, PLACES, TOK, HEAD), BF),
            pltpu.VMEM((HEADS // 2, PLACES, TOK, HEAD), BF),
            pltpu.VMEM((PLACES, TOK, D), BF),
            pltpu.VMEM((PLACES, HEADS, ROWS, HEAD), BF),
            pltpu.VMEM((PARTS, CHIPS, 64, HEAD), BF),
            pltpu.VMEM((PARTS, CHIPS, 64, HEAD), BF),
            pltpu.VMEM((PLACES * TOK, HW), BF),
            dma((PLACES + 2,)), dma((2,)),
            dma((PLACES,)), dma((PLACES,)), dma((PLACES,)), dma((PLACES,)), dma, dma,
            dma((PLACES,)), dma((PLACES,)), dma((PLACES,)), dma((PLACES,)), dma, dma,
            dma((PLACES,)), dma((PLACES,)), dma((PARTS, 6)), dma((PARTS, 6)),
        ],
        compiler_params=pltpu.CompilerParams(
            collective_id=0, has_side_effects=True, vmem_limit_bytes=62 * 1024 * 1024
        ),
        name="video_attention",
    )(dest_group, clip_blocks, text_count, qkv, text_kv, grad_out, out_weight)


def solution(mesh):
    return jax.shard_map(
        on_device,
        mesh=mesh,
        in_specs=(
            P("grp", "seq", None),
            P("grp", "seq", None),
            P(),
            P(),
            P(),
            P(),
            P("grp", "seq", None),
        ),
        out_specs=(
            P("grp", "seq", None),
            P("grp", "seq", None),
            P("grp", "seq", None),
            P("seq", "grp"),
        ),
        check_vma=False,
    )
```

time: 377 us -> 233 us (0.62)
  waiting for transfers between devices: 148 us -> 0 us
  Pallas kernels: 130 us -> 226 us
  blocking collectives: 27.9 us -> 0 us
  local copies, waits for them, and re-layouts: 30.4 us -> 5.95 us
  matrix products: 16.1 us -> 0 us
  between operations: 14.1 us -> 0.65 us
  starting transfers between devices: 7.63 us -> 0 us
    reduce_scatter x1 -> x0, waiting for transfers between devices: 128 us -> none  [on_device(): lax.psum_scatter(jnp.einsum('tr,td->rd', attended_rows, grad_rows, prefer...]
    pallas_call x2 -> x1, Pallas kernels: 130 us -> 226 us  [on_device(): pl.pallas_call(kernel, out_shape=(jax.ShapeDtypeStruct((PLACES, TOK, D),...]
    all_to_all x1 -> x0, blocking collectives: 27.9 us -> none  [on_device(): lax.all_to_all(attended[:, :, None, :], 'seq', split_axis=1, concat_axis=...]
    dot_general x2 -> x0, matrix products: 16.1 us -> none  [the longest x1 9.55 us: on_device(): jnp.dot(attended_rows, out_weight, preferred_element_type=F32).astype(BF)]
    unnamed x3 -> x0, waiting for transfers between devices: 13.9 us -> none
    reshape x2 -> x0, local copies, waits for them, and re-layouts: 7.69 us -> none  [the longest x1 5.63 us: on_device(): back_video.reshape(PLACES, TOK, 3 * HW)]
    all_to_all x2 -> x0, starting transfers between devices: 7.37 us -> none  [the longest x1 3.8 us: on_device(): lax.all_to_all(grad_video, 'seq', split_axis=1, concat_axis=3, tiled=True)]
    all_to_all x3 -> x0, local copies, waits for them, and re-layouts: 6.52 us -> none  [the longest x1 3.67 us: on_device(): lax.all_to_all(grad_video, 'seq', split_axis=1, concat_axis=3, tiled=True)]
  transfers between devices with their start and end apart: 4 -> 0, of which waited for: 3 -> 0; matrix products, arithmetic and copies ran while one was open for 9% -> 0% of each run, Pallas kernels for 0% -> 0%
where the time goes in v3:
time: 233 us; the launch traced here: 232 us
  Pallas kernels  226 us (97%)
  local copies, waits for them, and re-layouts  5.95 us (3%)
    pallas_call x1, Pallas kernels, on_device(): pl.pallas_call(kernel, out_shape=(jax.ShapeDtypeStruct((PLACES, TOK, D),...  226 us
    unnamed x10, local copies, waits for them, and re-layouts  5.95 us

profile of v3, /device:TPU:0, one launch (start us, length us, event | category | flops | bytes accessed | tf_op | source)
XLA Modules:
  0.0 232.1 jit_solution(12661000194407363491)
XLA Ops:
  0.6 225.5 %video_attention.1 = (bf16[4,64,3072]{2,1,0:T(8,128)(2,1)}, bf16[4,64,6144]{2,1,0:T(8,128)(2,1)}, bf16[4,16,4096]{2,1,0:T(8,128)(2,1)}, f32[128,384]{1,0:T(8,128)}) custom-call(s32[32]{0:T(128)} %dest_ref.1, s32[32]{0:T(128)} %blocks_ref.1, s32[32]{0:T(128)} %count_ref.1, bf16[4,64,6144]{2,1,0:T(8,128)(2,1)} %qkv_hbm.1, bf16[4,16,4096]{2,1,0:T(8,128)(2,1)} %text_hbm.1, ...), custom_call_target="tpu_custom_call" | custom-call | tf_op jit(solution)/shard_map/video_attention/pallas_call | solution.py:482
  226.1 0.0 copy-start
  226.2 2.8 %copy.15 = bf16[4,64,3072]{2,1,0:T(8,128)(2,1)} copy(bf16[4,64,3072]{2,1,0:T(8,128)(2,1)} %get-tuple-element.8) | data formatting | bytes 3145728
  229.0 0.0 copy-done
  229.0 0.0 copy-start.1
  229.0 0.0 copy-start.2
  229.0 1.7 copy.16
  230.6 0.0 copy-done.1
  230.6 0.8 copy.17
  231.4 0.0 copy-done.2
  231.4 0.7 copy.18
Async XLA Ops:
  226.1 2.8 %copy-start = (bf16[4,64,6144]{2,1,0:T(8,128)(2,1)S(1)}, bf16[4,64,6144]{2,1,0:T(8,128)(2,1)}, u32[]{:S(2)}) copy-start(bf16[4,64,6144]{2,1,0:T(8,128)(2,1)} %get-tuple-element.9) | copy-start | bytes 9437188
  229.0 1.7 copy-start.1
  229.0 2.5 %copy-start.2 = (f32[128,384]{1,0:T(8,128)S(1)}, f32[128,384]{1,0:T(8,128)}, u32[]{:S(2)}) copy-start(f32[128,384]{1,0:T(8,128)} %get-tuple-element.11) | copy-start | bytes 589828

commit v4 on v3

--- a/solution.py
+++ b/solution.py
@@ -47,8 +47,10 @@
     return found
 
 
-def relay_group(seat):
-    return lax.rem(seat, 2) * 4 + lax.rem(seat // 2, 4)
+def group_at(z_lo, by_place, by_dest, parity):
+    b1 = by_place + parity * (by_dest - by_place)
+    b2 = by_dest + parity * (by_place - by_dest)
+    return z_lo * 4 + b2 * 3 + (1 - 2 * b2) * b1
 
 
 def enter():
@@ -125,7 +127,7 @@
 def kernel(
     dest_ref, blocks_ref, count_ref, qkv_hbm, text_hbm, grad_hbm, weight_hbm,
     out_ref, gq_ref, gt_ref, gw_ref,
-    pack, relay0, relay1, relay2, relay3, sorted_, landed, gpack, glanded,
+    pack, relay, sorted_, landed, gpack, glanded,
     wide, total, q_s, k_s, v_s, g_s, kt, vt, bias, o_s, dq_s, dk_s, dv_s,
     alanded, afwd, gpart, blanded, acc, arrived, rows,
     load_sem, wide_sem, send1, recv1, send2, recv2, send3, recv3,
@@ -134,11 +136,26 @@
     g, s = lax.axis_index("grp"), lax.axis_index("seq")
     core = lax.rem(s, 2)
     partner = lax.bitwise_xor(s, 1)
-    relays = (relay0, relay1, relay2, relay3)
-    relay = relay_group(s)
-    half = s // 8
-    home = relay == g
+    z_lo = g // 4
+    ring = ring_bits(lax.rem(g, 4))
+
+    def by_place(parity):
+        return ring[0] + parity * (ring[1] - ring[0])
+
+    def by_dest(parity):
+        return ring[1] + parity * (ring[0] - ring[1])
+
+    def place_of(parity):
+        return 2 * z_lo + by_place(parity)
+
+    place = place_of(core)
+    mix = by_dest(core)
+    home = mix == core
     away = jnp.logical_not(home)
+
+    def unit_group(t, dest_bit):
+        unit = lax.bitwise_xor(place, t)
+        return group_at(unit // 2, lax.rem(unit, 2), dest_bit, core)
 
     def head_columns(t, h):
         return pl.ds(pl.multiple_of(t * HW + h * HEAD, HEAD), HEAD)
@@ -164,62 +181,62 @@
     widen(1).start()
     enter()
 
-    def push(j, h):
+    def push(t, h):
+        parity = lax.rem(h, 2)
+        j = lax.bitwise_xor(place_of(parity), t)
         return pltpu.make_async_remote_copy(
-            src_ref=pack.at[j, h], dst_ref=relays[j].at[g, half],
-            send_sem=send1.at[j], recv_sem=recv1.at[j],
-            device_id=(relay, h), device_id_type=MESH,
-        )
-
-    def spread(j):
-        loads[j].wait()
-
+            src_ref=pack.at[t, h], dst_ref=relay.at[g, s // 2],
+            send_sem=send1.at[t], recv_sem=recv1,
+            device_id=(group_at(j // 2, lax.rem(j, 2), core, parity), h), device_id_type=MESH,
+        )
+
+    def spread(t):
         def one(step, carry):
             h = lax.bitwise_xor(s, step)
-            for t in range(3):
-                pack[j, h, t * TOK:(t + 1) * TOK, :] = gq_ref[j, :, head_columns(t, h)]
-            for t in range(2):
-                at = 3 * TOK + t * TXT_DEV
-                pack[j, h, at:at + TXT_DEV, :] = gt_ref[j, :, head_columns(t, h)]
-
-            @pl.when(jnp.logical_or(step > 0, away))
+            j = lax.bitwise_xor(place_of(lax.rem(h, 2)), t)
+            for i in range(3):
+                pack[t, h, i * TOK:(i + 1) * TOK, :] = gq_ref[j, :, head_columns(i, h)]
+            for i in range(2):
+                at = 3 * TOK + i * TXT_DEV
+                pack[t, h, at:at + TXT_DEV, :] = gt_ref[j, :, head_columns(i, h)]
+
+            @pl.when(jnp.logical_or(step + t > 0, away))
             def _():
-                push(j, h).start()
+                push(t, h).start()
 
             return carry
 
         lax.fori_loop(0, HEADS, one, 0)
+        if t == 0:
+            @pl.when(home)
+            def _():
+                pltpu.make_async_copy(pack.at[0, s], relay.at[g, s // 2], recv1).start()
+
+    def spread_done(t):
+        if t > 0:
+            wait_for(pack.at[t], send1.at[t])
+            return
 
         @pl.when(home)
         def _():
-            pltpu.make_async_copy(pack.at[j, s], relays[j].at[g, half], recv1.at[j]).start()
-
-    def spread_done(j):
-        @pl.when(home)
-        def _():
-            wait_for(pack.at[j, pl.ds(1, HEADS - 1)], send1.at[j])
+            wait_for(pack.at[0, pl.ds(1, HEADS - 1)], send1.at[0])
 
         @pl.when(away)
         def _():
-            wait_for(pack.at[j], send1.at[j])
-
-    def regroup(j):
-        wait_for(relays[j], recv1.at[j])
-        if j >= 2:
-            wait_for(sorted_.at[j % 2, pl.ds(1, GROUPS - 1)], send2.at[j - 2])
-
-        def one(step, carry):
-            d = lax.bitwise_xor(g, step)
-            sorted_[j % 2, step] = relays[j][source_group(dest_ref, d, j)]
+            wait_for(pack.at[0], send1.at[0])
+
+    def regroup():
+        wait_for(relay, recv1)
+        neighbour = group_at(z_lo, by_place(core), 1 - mix, core)
+        for t in range(PLACES):
+            sorted_[t] = relay[source_group(dest_ref, unit_group(t, 1 - mix), place)]
             pltpu.make_async_remote_copy(
-                src_ref=sorted_.at[j % 2, step], dst_ref=landed.at[j, g],
-                send_sem=send2.at[j], recv_sem=recv2.at[j],
-                device_id=(d, s), device_id_type=MESH,
+                src_ref=sorted_.at[t], dst_ref=landed.at[t, mix],
+                send_sem=send2, recv_sem=recv2.at[t],
+                device_id=(neighbour, s), device_id_type=MESH,
             ).start()
-            return carry
-
-        lax.fori_loop(1, GROUPS, one, 0)
-        landed[j, g] = relays[j][source_group(dest_ref, g, j)]
+        for t in range(PLACES):
+            landed[t, mix] = relay[source_group(dest_ref, unit_group(t, mix), place)]
 
     def project_grads():
         for c in range(D // COLUMNS):
@@ -238,30 +255,36 @@
                     total[j * TOK:(j + 1) * TOK, h * HEAD:(h + 1) * HEAD] * live
                 ).astype(BF)
 
-        def one(step, carry):
-            h = lax.bitwise_xor(s, step)
-            pltpu.make_async_remote_copy(
-                src_ref=gpack.at[h], dst_ref=glanded.at[s], send_sem=send3, recv_sem=recv3,
-                device_id=(g, h), device_id_type=MESH,
-            ).start()
-            return carry
-
-        lax.fori_loop(1, HEADS, one, 0)
-        glanded[s] = gpack[s]
-
-    def attend(j):
-        wait_for(landed.at[j, pl.ds(1, GROUPS - 1)], recv2.at[j])
+        for t in range(PLACES):
+            def one(step, carry):
+                h = lax.bitwise_xor(s, step)
+                parity = lax.rem(h, 2)
+                j = lax.bitwise_xor(place_of(parity), t)
+                owner = group_at(j // 2, lax.rem(j, 2), by_dest(parity), parity)
+                pltpu.make_async_remote_copy(
+                    src_ref=gpack.at[h, j], dst_ref=glanded.at[t, s], send_sem=send3,
+                    recv_sem=recv3.at[t], device_id=(owner, h), device_id_type=MESH,
+                ).start()
+                return carry
+
+            lax.fori_loop(1 if t == 0 else 0, HEADS, one, 0)
+        glanded[0, s] = gpack[s, place]
+
+    def attend(t):
+        low = 1 if t == 0 else 0
+        wait_for(glanded.at[t, pl.ds(low, HEADS - low)], recv3.at[t])
+        wait_for(sorted_.at[t], recv2.at[t])
         for r in range(HEADS):
-            m, z = (r % 2) * 4 + (r // 2) % 4, r // 8
             here = slice(r * TOK, (r + 1) * TOK)
             text = slice(VIDEO + r * TXT_DEV, VIDEO + (r + 1) * TXT_DEV)
-            q_s[here, :] = landed[j, m, z, 0:TOK, :]
-            k_s[here, :] = landed[j, m, z, TOK:2 * TOK, :]
-            v_s[here, :] = landed[j, m, z, 2 * TOK:3 * TOK, :]
-            k_s[text, :] = landed[j, m, z, 3 * TOK:3 * TOK + TXT_DEV, :]
-            v_s[text, :] = landed[j, m, z, 3 * TOK + TXT_DEV:ROWS, :]
-            g_s[here, :] = glanded[r, j]
-        clip = source_group(dest_ref, g, j) * PLACES + j
+            q_s[here, :] = landed[t, r % 2, r // 2, 0:TOK, :]
+            k_s[here, :] = landed[t, r % 2, r // 2, TOK:2 * TOK, :]
+            v_s[here, :] = landed[t, r % 2, r // 2, 2 * TOK:3 * TOK, :]
+            k_s[text, :] = landed[t, r % 2, r // 2, 3 * TOK:3 * TOK + TXT_DEV, :]
+            v_s[text, :] = landed[t, r % 2, r // 2, 3 * TOK + TXT_DEV:ROWS, :]
+            g_s[here, :] = glanded[t, r]
+        dest = unit_group(t, mix)
+        clip = source_group(dest_ref, dest, place) * PLACES + place
         blocks = blocks_ref[clip]
         count = count_ref[clip]
         kt[...] = k_s[...].T
@@ -284,7 +307,7 @@
             e = jnp.exp2((st - top) * (SCALE * LOG2E))
             w = e * (1.0 / jnp.sum(e, axis=0, keepdims=True))
             wb = w.astype(BF)
-            o_s[j, at, :] = (dot_nn(vt[...], wb) * live).T.astype(BF)
+            o_s[t, at, :] = (dot_nn(vt[...], wb) * live).T.astype(BF)
             dv_s[...] += dot_nn(wb, gr)
             dp = dot_nt(v_s[...], gr)
             centre = jnp.sum(dp * w, axis=0, keepdims=True)
@@ -298,60 +321,68 @@
         def send_att(step, carry):
             r = lax.bitwise_xor(s, step)
             pltpu.make_async_remote_copy(
-                src_ref=o_s.at[j, token_rows(r), :], dst_ref=alanded.at[s, j],
-                send_sem=asend.at[j], recv_sem=arecv.at[j], device_id=(g, r), device_id_type=MESH,
+                src_ref=o_s.at[t, token_rows(r), :], dst_ref=alanded.at[s, place],
+                send_sem=asend.at[t], recv_sem=arecv.at[t],
+                device_id=(dest, r), device_id_type=MESH,
             ).start()
             return carry
 
-        lax.fori_loop(1, HEADS, send_att, 0)
-        alanded[s, j] = o_s[j, token_rows(s), :]
-        spread_done(j)
+        lax.fori_loop(low, HEADS, send_att, 0)
+        if t == 0:
+            alanded[s, place] = o_s[t, token_rows(s), :]
+        spread_done(t)
 
         def send_back(step, carry):
             r = lax.bitwise_xor(s, step)
-            pack[j, r, 0:TOK, :] = dq_s[token_rows(r), :]
-            pack[j, r, TOK:2 * TOK, :] = dk_s[token_rows(r), :].astype(BF)
-            pack[j, r, 2 * TOK:3 * TOK, :] = dv_s[token_rows(r), :].astype(BF)
-            pack[j, r, 3 * TOK:3 * TOK + TXT_DEV, :] = dk_s[text_rows(r), :].astype(BF)
-            pack[j, r, 3 * TOK + TXT_DEV:ROWS, :] = dv_s[text_rows(r), :].astype(BF)
-
-            @pl.when(step > 0)
+            pack[t, r, 0:TOK, :] = dq_s[token_rows(r), :]
+            pack[t, r, TOK:2 * TOK, :] = dk_s[token_rows(r), :].astype(BF)
+            pack[t, r, 2 * TOK:3 * TOK, :] = dv_s[token_rows(r), :].astype(BF)
+            pack[t, r, 3 * TOK:3 * TOK + TXT_DEV, :] = dk_s[text_rows(r), :].astype(BF)
+            pack[t, r, 3 * TOK + TXT_DEV:ROWS, :] = dv_s[text_rows(r), :].astype(BF)
+
+            @pl.when(step >= low)
             def _():
                 pltpu.make_async_remote_copy(
-                    src_ref=pack.at[j, r], dst_ref=blanded.at[j, s],
-                    send_sem=bsend.at[j], recv_sem=brecv.at[j],
-                    device_id=(g, r), device_id_type=MESH,
+                    src_ref=pack.at[t, r], dst_ref=blanded.at[t, s],
+                    send_sem=bsend.at[t], recv_sem=brecv.at[t],
+                    device_id=(dest, r), device_id_type=MESH,
                 ).start()
 
             return carry
 
         lax.fori_loop(0, HEADS, send_back, 0)
-        blanded[j, s] = pack[j, s]
-
-    def forward(j):
-        wait_for(alanded.at[pl.ds(1, HEADS - 1), j], arecv.at[j])
+        if t == 0:
+            blanded[t, s] = pack[t, s]
+
+    def forward(t):
+        low = 1 if t == 0 else 0
+        wait_for(alanded.at[pl.ds(low, HEADS - low), t], arecv.at[t])
+        lent = lax.bitwise_xor(place_of(1 - core), t)
 
         def one(i, carry):
             pltpu.make_async_remote_copy(
-                src_ref=alanded.at[2 * i + 1 - core, j], dst_ref=afwd.at[i, j],
-                send_sem=fsend.at[j], recv_sem=frecv.at[j],
+                src_ref=alanded.at[2 * i + 1 - core, lent], dst_ref=afwd.at[i, lent],
+                send_sem=fsend.at[t], recv_sem=frecv.at[t],
                 device_id=(g, partner), device_id_type=MESH,
             ).start()
             return carry
 
         lax.fori_loop(0, HEADS // 2, one, 0)
         for h in range(HEADS):
-            rows[j * TOK:(j + 1) * TOK, h * HEAD:(h + 1) * HEAD] = alanded[h, j]
-
-    def collect(j):
-        wait_for(blanded.at[j, pl.ds(1, HEADS - 1)], brecv.at[j])
+            j = lax.bitwise_xor(place_of(h % 2), t)
+            rows[token_rows(j), h * HEAD:(h + 1) * HEAD] = alanded[h, j]
+
+    def collect(t):
+        low = 1 if t == 0 else 0
+        wait_for(blanded.at[t, pl.ds(low, HEADS - low)], brecv.at[t])
 
         def one(h, carry):
-            for t in range(3):
-                gq_ref[j, :, head_columns(t, h)] = blanded[j, h, t * TOK:(t + 1) * TOK, :]
-            for t in range(2):
-                at = 3 * TOK + t * TXT_DEV
-                gt_ref[j, :, head_columns(t, h)] = blanded[j, h, at:at + TXT_DEV, :]
+            j = lax.bitwise_xor(place_of(lax.rem(h, 2)), t)
+            for i in range(3):
+                gq_ref[j, :, head_columns(i, h)] = blanded[t, h, i * TOK:(i + 1) * TOK, :]
+            for i in range(2):
+                at = 3 * TOK + i * TXT_DEV
+                gt_ref[j, :, head_columns(i, h)] = blanded[t, h, at:at + TXT_DEV, :]
             return carry
 
         lax.fori_loop(0, HEADS, one, 0)
@@ -417,9 +448,10 @@
                     1.0 / (PLACES * GROUPS)
                 )
 
-    loads[PLACES].wait()
-    spread(0)
-    spread(1)
+    for load in loads[:PLACES + 1]:
+        load.wait()
+    for t in range(PLACES):
+        spread(t)
     loads[PLACES + 1].wait()
     lend = pltpu.make_async_remote_copy(
         src_ref=out_ref, dst_ref=gpart, send_sem=lend_send, recv_sem=lend_recv,
@@ -427,15 +459,9 @@
     )
     lend.start()
     project_grads()
-    regroup(0)
-    spread(2)
-    regroup(1)
-    spread(3)
-    wait_for(glanded.at[pl.ds(1, HEADS - 1)], recv3)
+    regroup()
     attend(0)
-    regroup(2)
     attend(1)
-    regroup(3)
     forward(0)
     attend(2)
     forward(1)
@@ -461,13 +487,14 @@
         reduce_stage(k)
     collect(3)
 
-    for j in range(PLACES):
-        if j >= 2:
-            wait_for(sorted_.at[j % 2, pl.ds(1, GROUPS - 1)], send2.at[j])
-        wait_for(o_s.at[j, pl.ds(TOK, VIDEO - TOK)], asend.at[j])
-        wait_for(afwd.at[:, j], fsend.at[j])
-        wait_for(pack.at[j, pl.ds(1, HEADS - 1)], bsend.at[j])
-    wait_for(gpack.at[pl.ds(1, HEADS - 1)], send3)
+    for t in range(PLACES):
+        low = 1 if t == 0 else 0
+        wait_for(o_s.at[t, pl.ds(low * TOK, VIDEO - low * TOK)], asend.at[t])
+        wait_for(afwd.at[:, t], fsend.at[t])
+        wait_for(pack.at[t, pl.ds(low, HEADS - low)], bsend.at[t])
+    wait_for(sorted_, send2)
+    wait_for(gpack.at[:, pl.ds(1, PLACES - 1)], send3)
+    wait_for(gpack.at[pl.ds(1, HEADS - 1), 0], send3)
     for k in range(6):
         for p in range(PARTS):
             exchange(p, k).wait_send()
@@ -478,7 +505,6 @@
     vmem = pl.BlockSpec(memory_space=pltpu.VMEM)
     hbm = pl.BlockSpec(memory_space=pl.ANY)
     dma = pltpu.SemaphoreType.DMA
-    relay = pltpu.VMEM((GROUPS, 2, ROWS, HEAD), BF)
     return pl.pallas_call(
         kernel,
         out_shape=(
@@ -491,11 +517,11 @@
         out_specs=(vmem,) * 4,
         scratch_shapes=[
             pltpu.VMEM((PLACES, HEADS, ROWS, HEAD), BF),
-            relay, relay, relay, relay,
-            pltpu.VMEM((2, GROUPS, 2, ROWS, HEAD), BF),
-            pltpu.VMEM((PLACES, GROUPS, 2, ROWS, HEAD), BF),
+            pltpu.VMEM((GROUPS, HEADS // 2, ROWS, HEAD), BF),
+            pltpu.VMEM((PLACES, HEADS // 2, ROWS, HEAD), BF),
+            pltpu.VMEM((PLACES, 2, HEADS // 2, ROWS, HEAD), BF),
             pltpu.VMEM((HEADS, PLACES, TOK, HEAD), BF),
-            pltpu.VMEM((HEADS, PLACES, TOK, HEAD), BF),
+            pltpu.VMEM((PLACES, HEADS, TOK, HEAD), BF),
             pltpu.VMEM((2, HW, COLUMNS), BF),
             pltpu.VMEM((PLACES * TOK, HW), F32),
             pltpu.VMEM((VIDEO, HEAD), BF),
@@ -517,7 +543,7 @@
             pltpu.VMEM((PARTS, CHIPS, 64, HEAD), BF),
             pltpu.VMEM((PLACES * TOK, HW), BF),
             dma((PLACES + 2,)), dma((2,)),
-            dma((PLACES,)), dma((PLACES,)), dma((PLACES,)), dma((PLACES,)), dma, dma,
+            dma((PLACES,)), dma, dma, dma((PLACES,)), dma, dma((PLACES,)),
             dma((PLACES,)), dma((PLACES,)), dma((PLACES,)), dma((PLACES,)), dma, dma,
             dma((PLACES,)), dma((PLACES,)), dma((PARTS, 6)), dma((PARTS, 6)),
         ],

time: 233 us -> 188 us (0.81)
  Pallas kernels: 226 us -> 181 us
    pallas_call x1, Pallas kernels: 226 us -> 181 us  [on_device(): pl.pallas_call(kernel, out_shape=(jax.ShapeDtypeStruct((PLACES, TOK, D),...]
where the time goes in v4:
time: 188 us
  Pallas kernels  181 us (96%)
  local copies, waits for them, and re-layouts  5.95 us (3%)
    pallas_call x1, Pallas kernels, on_device(): pl.pallas_call(kernel, out_shape=(jax.ShapeDtypeStruct((PLACES, TOK, D),...  181 us
    unnamed x10, local copies, waits for them, and re-layouts  5.95 us

profile of v4, /device:TPU:0, one launch (start us, length us, event | category | flops | bytes accessed | tf_op | source)
XLA Modules:
  0.0 187.8 jit_solution(17108226919713810469)
XLA Ops:
  0.6 181.2 %video_attention.1 = (bf16[4,64,3072]{2,1,0:T(8,128)(2,1)}, bf16[4,64,6144]{2,1,0:T(8,128)(2,1)}, bf16[4,16,4096]{2,1,0:T(8,128)(2,1)}, f32[128,384]{1,0:T(8,128)}) custom-call(s32[32]{0:T(128)} %dest_ref.1, s32[32]{0:T(128)} %blocks_ref.1, s32[32]{0:T(128)} %count_ref.1, bf16[4,64,6144]{2,1,0:T(8,128)(2,1)} %qkv_hbm.1, bf16[4,16,4096]{2,1,0:T(8,128)(2,1)} %text_hbm.1, ...), custom_call_target="tpu_custom_call" | custom-call | tf_op jit(solution)/shard_map/video_attention/pallas_call | solution.py:508
  181.8 0.0 copy-start
  181.8 2.8 %copy.15 = bf16[4,64,3072]{2,1,0:T(8,128)(2,1)} copy(bf16[4,64,3072]{2,1,0:T(8,128)(2,1)} %get-tuple-element.8) | data formatting | bytes 3145728
  184.6 0.0 copy-done
  184.6 0.0 copy-start.1
  184.6 0.0 copy-start.2
  184.6 1.7 copy.16
  186.3 0.0 copy-done.1
  186.3 0.8 copy.17
  187.1 0.0 copy-done.2
  187.1 0.7 copy.18
Async XLA Ops:
  181.8 2.8 %copy-start = (bf16[4,64,6144]{2,1,0:T(8,128)(2,1)S(1)}, bf16[4,64,6144]{2,1,0:T(8,128)(2,1)}, u32[]{:S(2)}) copy-start(bf16[4,64,6144]{2,1,0:T(8,128)(2,1)} %get-tuple-element.9) | copy-start | bytes 9437188
  184.6 1.7 copy-start.1
  184.6 2.5 %copy-start.2 = (f32[128,384]{1,0:T(8,128)S(1)}, f32[128,384]{1,0:T(8,128)}, u32[]{:S(2)}) copy-start(f32[128,384]{1,0:T(8,128)} %get-tuple-element.11) | copy-start | bytes 589828
